TPU v7x, 512 devices: a whole 4x4x16 slice. The times are simulated.
512 devices in a mesh: lon: 64 (over z, x_hi, core), lat: 8 (over x_lo, y).
Axes of the slice: x: 4 (x_hi: 2, x_lo: 2; x = x_hi * 2 + x_lo), y: 4, z: 16, core: 2. Of those that a mesh axis runs over, the one named last changes fastest.
Arguments:
- patches: bfloat16 [2, 48, 1536, 512], P(None, 'lat', 'lon'), may hold values from -6 to 6
- regions: int32 [2, 48, 1536], P(None, 'lat', 'lon'), may hold values from 0 to 2, as said below
- w_qkv: bfloat16 [512, 1536], replicated, may hold values from -0.25 to 0.25
- w_out: bfloat16 [512, 512], replicated, may hold values from -1 to 1
Outputs:
- updated: bfloat16 [2, 48, 1536, 512], P(None, 'lat', 'lon')
Inputs may be any that keep to these rules, and one draw needn't show every extreme that they name: `regions`: constant over aligned tiles of 3 latitude by 6 longitude patches, and the same at every level.
All inputs are finite; a program needn't handle non-finite values.
Results may differ from a plain program's by a relative error of at most 0.0065.
Values may be sent and summed in bfloat16 or wider, within the bound.
A program may use at most 64 MiB of HBM per device.

v0:
```python
import math

import jax
import jax.numpy as jnp
from jax import lax
from jax.sharding import PartitionSpec as P

HEADS = 16
WIN_H = 6
WIN_W = 12
SHIFT_H = 3
SHIFT_W = 6


def from_behind(value, axis, steps):
    count = lax.axis_size(axis)
    pairs = [(source, (source + steps) % count) for source in range(count)]
    return lax.ppermute(value, axis, pairs)


def layer_norm(source):
    values = source.astype(jnp.float32)
    center = values - jnp.mean(values, axis=-1, keepdims=True)
    spread = jnp.mean(center * center, axis=-1, keepdims=True)
    return (center * lax.rsqrt(spread + 1e-05)).astype(jnp.bfloat16)


def to_windows(source):
    levels, row_count, col_count, feature_count = source.shape
    source = source.reshape(
        levels, row_count // WIN_H, WIN_H, col_count // WIN_W, WIN_W, feature_count
    )
    source = source.transpose(1, 3, 0, 2, 4, 5)
    return source.reshape(
        row_count // WIN_H, col_count // WIN_W, levels * WIN_H * WIN_W, feature_count
    )


def from_windows(source, levels, row_count, col_count):
    feature_count = source.shape[-1]
    source = source.reshape(
        row_count // WIN_H, col_count // WIN_W, levels, WIN_H, WIN_W, feature_count
    )
    source = source.transpose(2, 0, 3, 1, 4, 5)
    return source.reshape(levels, row_count, col_count, feature_count)


def attend(window_block, region_ids, polar_rows, w_qkv):
    levels, row_count, col_count, width = window_block.shape
    normed = layer_norm(window_block)
    projected = jnp.dot(
        normed.reshape(-1, width), w_qkv, preferred_element_type=jnp.float32
    ).astype(jnp.bfloat16)
    projected = to_windows(projected.reshape(levels, row_count, col_count, 3 * width))
    labels = to_windows(region_ids[..., None])[..., 0]
    pole_class = to_windows(
        jnp.broadcast_to(polar_rows[None, :, None, None], (levels, row_count, col_count, 1))
    )[..., 0]
    head_depth = width // HEADS

    def one_band(pieces):
        band_qkv, band_labels, band_poles = pieces
        window_count, window_size = (band_qkv.shape[0], band_qkv.shape[1])
        queries = band_qkv[..., :width].reshape(window_count, window_size, HEADS, head_depth)
        key_vecs = band_qkv[..., width : 2 * width].reshape(
            window_count, window_size, HEADS, head_depth
        )
        values = band_qkv[..., 2 * width :].reshape(window_count, window_size, HEADS, head_depth)
        visible = (band_labels[:, :, None] == band_labels[:, None, :]) & (
            band_poles[:, :, None] == band_poles[:, None, :]
        )
        scores = jnp.einsum(
            "wqhd,wkhd->whqk", queries, key_vecs, preferred_element_type=jnp.float32
        ) * (1.0 / math.sqrt(head_depth))
        weights = jnp.where(visible[:, None], jnp.exp(scores), jnp.float32(0.0))
        weights = (weights / jnp.sum(weights, axis=-1, keepdims=True)).astype(jnp.bfloat16)
        result = jnp.einsum("whqk,wkhd->wqhd", weights, values, preferred_element_type=jnp.float32)
        return result.astype(jnp.bfloat16).reshape(window_count, window_size, width)

    attended = lax.map(one_band, (projected, labels, pole_class))
    return from_windows(attended, levels, row_count, col_count)


def shards(patches, regions, w_qkv, w_out):
    levels, row_count, col_count, width = patches.shape
    lat_index = lax.axis_index("lat")
    height = row_count * lax.axis_size("lat")
    arrived = from_behind((patches[:, :, :SHIFT_W], regions[:, :, :SHIFT_W]), "lon", -1)
    wider = jnp.concatenate([patches, arrived[0]], axis=2)
    wider_ids = jnp.concatenate([regions, arrived[1]], axis=2)
    arrived = from_behind((wider[:, :SHIFT_H], wider_ids[:, :SHIFT_H]), "lat", -1)
    shifted = jnp.concatenate([wider, arrived[0]], axis=1)[:, SHIFT_H:, SHIFT_W:]
    shifted_ids = jnp.concatenate([wider_ids, arrived[1]], axis=1)[:, SHIFT_H:, SHIFT_W:]
    global_rows = lat_index * row_count + jnp.arange(row_count, dtype=jnp.int32)
    polar_rows = (global_rows >= height - SHIFT_H).astype(jnp.int32)
    result = attend(shifted, shifted_ids, polar_rows, w_qkv)
    moved = from_behind(result[:, :, col_count - SHIFT_W :], "lon", 1)
    aligned = jnp.concatenate([moved, result[:, :, : col_count - SHIFT_W]], axis=2)
    moved = from_behind(aligned[:, row_count - SHIFT_H :], "lat", 1)
    attended = jnp.concatenate([moved, aligned[:, : row_count - SHIFT_H]], axis=1)
    output = jnp.dot(attended.reshape(-1, width), w_out, preferred_element_type=jnp.float32)
    return (patches.astype(jnp.float32) + output.reshape(patches.shape)).astype(jnp.bfloat16)


def solution(mesh):
    return jax.shard_map(
        shards,
        mesh=mesh,
        in_specs=(P(None, "lat", "lon", None), P(None, "lat", "lon"), P(), P()),
        out_specs=P(None, "lat", "lon", None),
        check_vma=False,
    )
```

profile of v0, /device:TPU:2, one launch (start us, length us, event | category | flops | bytes accessed | tf_op | source)
XLA Modules:
  0.0 70.4 jit_solution(1066603170090725670)
XLA Ops:
  0.0 1.0 %slice.42 = bf16[2,6,6,512]{3,2,1,0:T(8,128)(2,1)S(1)} slice(bf16[2,6,24,512]{3,2,1,0:T(8,128)(2,1)} %param.4), slice={[0:2], [0:6], [0:6], [0:512]} | slice | bytes 147456 | tf_op jit(solution)/shard_map/slice | solution.py:88
  1.0 12.4 %collective-permute-start = (bf16[2,6,6,512]{3,2,1,0:T(8,128)(2,1)S(1)}, bf16[2,6,6,512]{3,2,1,0:T(8,128)(2,1)S(1)}, u32[]{:S(2)}, u32[]{:S(2)}) collective-permute-start(bf16[2,6,6,512]{3,2,1,0:T(8,128)(2,1)S(1)} %slice.42), channel_id=1, source_target_pairs={{0,504},{8,0},{16,8},{24,16},{32,24},{40,32},{48,40},{56,48},{64,5... | collective-permute-start | bytes 221192 | tf_op jit(solution)/shard_map/ppermute | solution.py:18
  13.4 2.6 %collective-permute-start.2 = (s32[2,6,6]{2,0,1:T(2,128)}, s32[2,6,6]{2,0,1:T(2,128)S(1)}, u32[]{:S(2)}, u32[]{:S(2)}) collective-permute-start(s32[2,6,6]{2,0,1:T(2,128)} %bitcast.42), channel_id=1, source_target_pairs={{0,504},{8,0},{16,8},{24,16},{32,24},{40,32},{48,40},{56,48},{64,5... | collective-permute-start | bytes 872 | tf_op jit(solution)/shard_map/ppermute | solution.py:18
  16.0 1.0 %constant_dynamic-update-slice_fusion.1 = bf16[2,6,30,512]{3,2,1,0:T(8,128)(2,1)S(1)} fusion(bf16[2,6,24,512]{3,2,1,0:T(8,128)(2,1)} %param.4), kind=kLoop, calls=%fused_computation.30 | loop fusion | bytes 589824
  17.0 0.5 collective-permute-done.2
  17.6 0.8 %pad_add_fusion.2 = s32[2,3,30]{2,0,1:T(2,128)S(1)} fusion(s32[2,6,6]{2,0,1:T(2,128)S(1)} %collective-permute-done.2, s32[2,6,24]{2,0,1:T(2,128)} %param.5), kind=kLoop, calls=%fused_computation.32 | loop fusion | flops 180 | bytes 2160 | tf_op jit(solution)/shard_map/concatenate | solution.py:90
  18.3 5.8 %collective-permute-start.3 = (s32[2,3,30]{2,0,1:T(2,128)S(1)}, s32[2,3,30]{2,0,1:T(2,128)S(1)}, u32[]{:S(2)}, u32[]{:S(2)}) collective-permute-start(s32[2,3,30]{2,0,1:T(2,128)S(1)} %pad_add_fusion.2), channel_id=1, source_target_pairs={{0,7},{1,0},{2,1},{3,2},{4,3},{5,4},{6,5},{7,6},{8,15},{9,8},{10,9... | collective-permute-start | bytes 2168 | tf_op jit(solution)/shard_map/ppermute | solution.py:18
  24.3 1.1 %collective-permute-done.3 = s32[2,3,30]{2,0,1:T(2,128)S(1)} collective-permute-done((s32[2,3,30]{2,0,1:T(2,128)S(1)}, s32[2,3,30]{2,0,1:T(2,128)S(1)}, u32[]{:S(2)}, u32[]{:S(2)}) %collective-permute-start.3) | collective-permute-done | bytes 752 | tf_op jit(solution)/shard_map/ppermute | solution.py:18
  25.4 0.8 %pad_add_fusion = s32[2,6,24]{2,0,1:T(2,128)S(1)} fusion(s32[2,3,30]{2,0,1:T(2,128)S(1)} %collective-permute-done.3, s32[2,6,6]{2,0,1:T(2,128)S(1)} %collective-permute-done.2, s32[2,6,24]{2,0,1:T(2,128)} %param.5), kind=kLoop, calls=%fused_computation.27 | loop fusion | flops 576 | bytes 3312 | tf_op jit(solution)/shard_map/concatenate | solution.py:93
  26.4 6.3 %collective-permute-start.1 = (bf16[2,3,30,512]{3,2,1,0:T(8,128)(2,1)S(1)}, bf16[2,3,30,512]{3,2,1,0:T(8,128)(2,1)S(1)}, u32[]{:S(2)}, u32[]{:S(2)}) collective-permute-start(bf16[2,3,30,512]{3,2,1,0:T(8,128)(2,1)S(1)} %slice.55), channel_id=1, source_target_pairs={{0,7},{1,0},{2,1},{3,2},{4,3},{5,4},{6,5},{7,6},{8,15},{9,8},{10,9... | collective-permute-start | bytes 552968 | tf_op jit(solution)/shard_map/ppermute | solution.py:18
  32.8 3.0 %collective-permute-done.1 = bf16[2,3,30,512]{3,2,1,0:T(8,128)(2,1)S(1)} collective-permute-done((bf16[2,3,30,512]{3,2,1,0:T(8,128)(2,1)S(1)}, bf16[2,3,30,512]{3,2,1,0:T(8,128)(2,1)S(1)}, u32[]{:S(2)}, u32[]{:S(2)}) %collective-permute-start.1) | collective-permute-done | bytes 184352 | tf_op jit(solution)/shard_map/ppermute | solution.py:18
  36.5 1.5 %convolution_convert_fusion = bf16[288,1536]{1,0:T(8,128)(2,1)} fusion(bf16[288,512]{1,0:T(8,128)(2,1)S(1)} %bitcast.40, bf16[512,1536]{1,0:T(8,128)(2,1)S(1)} %copy-done), kind=kOutput, calls=%fused_computation.3 | convolution fusion | flops 453427200 | bytes 2752512 | tf_op jit(solution)/shard_map/dot_general | solution.py:51
  38.1 1.3 %reshape_reshape.3 = bf16[2,1,6,2,12,1536]{5,4,3,2,0,1:T(8,128)(2,1)S(1)} reshape(bf16[288,1536]{1,0:T(8,128)(2,1)} %convolution_convert_fusion) | data formatting | bytes 1769472 | tf_op jit(solution)/shard_map/reshape;reshape | solution.py:30
  39.4 0.9 %copy.7 = bf16[1,2,2,6,12,1536]{5,1,4,3,2,0:T(2,128)(2,1)S(1)} copy(bf16[1,2,2,6,12,1536]{5,4,1,3,2,0:T(8,128)(2,1)S(1)} %bitcast.32) | data formatting | bytes 1769472 | tf_op jit(solution)/shard_map/transpose | solution.py:33
  40.3 0.6 fusion.18
  42.3 1.3 %fusion = (f32[2,16,144]{2,1,0:T(8,128)S(1)}, f32[2,16,144,144]{2,3,1,0:T(8,128)S(1)}) fusion(pred[2,144,144]{1,2,0:T(8,128)(4,1)S(1)} %compare_and_fusion, bf16[2,144,16,32]{1,3,2,0:T(8,128)(2,1)S(1)} %bitcast.37, bf16[2,144,16,32]{1,3,2,0:T(8,128)(2,1)S(1)} %bitcast.39), kind=kOutput, calls=%fused_computation.2 | convolution fusion | flops 44453376 | bytes 3303936 | tf_op jit(solution)/shard_map/while/body/eval_jaxpr/wqhd,wkhd->whqk/dot_general | solution.py:72
  43.6 2.0 %fusion.3 = bf16[2,144,16,32]{1,3,2,0:T(8,128)(2,1)} fusion(bf16[2,144,16,32]{1,3,2,0:T(8,128)(2,1)S(1)} %bitcast.38, f32[2,16,144,144]{2,3,1,0:T(8,128)S(1)} %get-tuple-element.24, f32[2,16,144]{2,1,0:T(8,128)S(1)} %get-tuple-element.22, pred[2,144,144]{1,2,0:T(8,128)(4,1)S(1)} %compare_and_fusion), kind=kOutput, calls=%fused_computation.7 | convolution fusion | flops 45268992 | bytes 3303936 | tf_op jit(solution)/shard_map/while/body/eval_jaxpr/whqk,wkhd->wqhd/dot_general | solution.py:77
  45.7 2.0 %copy.13 = bf16[2,144,16,32]{3,2,0,1:T(8,128)(2,1)S(1)} copy(bf16[2,144,16,32]{1,3,2,0:T(8,128)(2,1)} %fusion.3) | data formatting | bytes 589824 | tf_op jit(solution)/shard_map/while/body/eval_jaxpr/convert_element_type | solution.py:78
  47.7 0.9 %reshape.70 = bf16[1,2,2,6,12,512]{5,1,4,3,2,0:T(2,128)(2,1)S(1)} reshape(bf16[2,144,16,32]{3,2,0,1:T(8,128)(2,1)S(1)} %copy.13) | data formatting | bytes 589824 | tf_op jit(solution)/shard_map/reshape | solution.py:41
  49.0 1.9 %collective-permute-start.4 = (bf16[2,6,6,512]{3,2,1,0:T(8,128)(2,1)S(1)}, bf16[2,6,6,512]{3,2,1,0:T(8,128)(2,1)S(1)}, u32[]{:S(2)}, u32[]{:S(2)}) collective-permute-start(bf16[2,6,6,512]{3,2,1,0:T(8,128)(2,1)S(1)} %copy.19), channel_id=1, source_target_pairs={{0,8},{8,16},{16,24},{24,32},{32,40},{40,48},{48,56},{56,64},{64,7... | collective-permute-start | bytes 221192 | tf_op jit(solution)/shard_map/ppermute | solution.py:18
  51.1 7.4 %collective-permute-done.4 = bf16[2,6,6,512]{3,2,1,0:T(8,128)(2,1)S(1)} collective-permute-done((bf16[2,6,6,512]{3,2,1,0:T(8,128)(2,1)S(1)}, bf16[2,6,6,512]{3,2,1,0:T(8,128)(2,1)S(1)}, u32[]{:S(2)}, u32[]{:S(2)}) %collective-permute-start.4) | collective-permute-done | bytes 73760 | tf_op jit(solution)/shard_map/ppermute | solution.py:18
  58.6 1.9 %collective-permute-start.5 = (bf16[2,3,24,512]{3,2,1,0:T(8,128)(2,1)S(1)}, bf16[2,3,24,512]{3,2,1,0:T(8,128)(2,1)S(1)}, u32[]{:S(2)}, u32[]{:S(2)}) collective-permute-start(bf16[2,3,24,512]{3,2,1,0:T(8,128)(2,1)S(1)} %fusion.14), channel_id=1, source_target_pairs={{0,1},{1,2},{2,3},{3,4},{4,5},{5,6},{6,7},{7,0},{8,9},{9,10},{10,1... | collective-permute-start | bytes 442376 | tf_op jit(solution)/shard_map/ppermute | solution.py:18
  60.5 7.8 %collective-permute-done.5 = bf16[2,3,24,512]{3,2,1,0:T(8,128)(2,1)S(1)} collective-permute-done((bf16[2,3,24,512]{3,2,1,0:T(8,128)(2,1)S(1)}, bf16[2,3,24,512]{3,2,1,0:T(8,128)(2,1)S(1)}, u32[]{:S(2)}, u32[]{:S(2)}) %collective-permute-start.5) | collective-permute-done | bytes 147488 | tf_op jit(solution)/shard_map/ppermute | solution.py:18
  68.3 2.1 %fusion.4 = bf16[2,6,24,512]{3,2,1,0:T(8,128)(2,1)} fusion(bf16[2,6,24,512]{3,2,1,0:T(8,128)(2,1)S(1)} %copy-done.1, bf16[512,512]{1,0:T(8,128)(2,1)} %param.7, bf16[2,6,18,512]{3,2,1,0:T(8,128)(2,1)S(1)} %copy.20, bf16[2,6,6,512]{3,2,1,0:T(8,128)(2,1)S(1)} %collective-permute-done.4, bf16[2,3,24,512]{3,2,1,0:T(8,128)(2,1)S(1)} %collective-permute-done.5), kind=kOutput, calls=%fused_computation.8 | convolution fusion | flops 152322048 | bytes 1556480 | tf_op jit(solution)/shard_map/dot_general | solution.py:101
  (28 shorter events, 3.1 us)
Async XLA Ops:
  0.0 36.5 %copy-start = (bf16[512,1536]{1,0:T(8,128)(2,1)S(1)}, bf16[512,1536]{1,0:T(8,128)(2,1)}, u32[]{:S(2)}) copy-start(bf16[512,1536]{1,0:T(8,128)(2,1)} %param.6) | copy-start | bytes 4718596
  1.0 25.3 %collective-permute-start = (bf16[2,6,6,512]{3,2,1,0:T(8,128)(2,1)S(1)}, bf16[2,6,6,512]{3,2,1,0:T(8,128)(2,1)S(1)}, u32[]{:S(2)}, u32[]{:S(2)}) collective-permute-start(bf16[2,6,6,512]{3,2,1,0:T(8,128)(2,1)S(1)} %slice.42), channel_id=1, source_target_pairs={{0,504},{8,0},{16,8},{24,16},{32,24},{40,32},{48,40},{56,48},{64,5... | collective-permute-start | bytes 221192 | tf_op jit(solution)/shard_map/ppermute | solution.py:18
  13.4 4.1 %collective-permute-start.2 = (s32[2,6,6]{2,0,1:T(2,128)}, s32[2,6,6]{2,0,1:T(2,128)S(1)}, u32[]{:S(2)}, u32[]{:S(2)}) collective-permute-start(s32[2,6,6]{2,0,1:T(2,128)} %bitcast.42), channel_id=1, source_target_pairs={{0,504},{8,0},{16,8},{24,16},{32,24},{40,32},{48,40},{56,48},{64,5... | collective-permute-start | bytes 872 | tf_op jit(solution)/shard_map/ppermute | solution.py:18
  18.3 7.1 %collective-permute-start.3 = (s32[2,3,30]{2,0,1:T(2,128)S(1)}, s32[2,3,30]{2,0,1:T(2,128)S(1)}, u32[]{:S(2)}, u32[]{:S(2)}) collective-permute-start(s32[2,3,30]{2,0,1:T(2,128)S(1)} %pad_add_fusion.2), channel_id=1, source_target_pairs={{0,7},{1,0},{2,1},{3,2},{4,3},{5,4},{6,5},{7,6},{8,15},{9,8},{10,9... | collective-permute-start | bytes 2168 | tf_op jit(solution)/shard_map/ppermute | solution.py:18
  26.4 9.5 %collective-permute-start.1 = (bf16[2,3,30,512]{3,2,1,0:T(8,128)(2,1)S(1)}, bf16[2,3,30,512]{3,2,1,0:T(8,128)(2,1)S(1)}, u32[]{:S(2)}, u32[]{:S(2)}) collective-permute-start(bf16[2,3,30,512]{3,2,1,0:T(8,128)(2,1)S(1)} %slice.55), channel_id=1, source_target_pairs={{0,7},{1,0},{2,1},{3,2},{4,3},{5,4},{6,5},{7,6},{8,15},{9,8},{10,9... | collective-permute-start | bytes 552968 | tf_op jit(solution)/shard_map/ppermute | solution.py:18
  45.7 22.6 %copy-start.1 = (bf16[2,6,24,512]{3,2,1,0:T(8,128)(2,1)S(1)}, bf16[2,6,24,512]{3,2,1,0:T(8,128)(2,1)}, u32[]{:S(2)}) copy-start(bf16[2,6,24,512]{3,2,1,0:T(8,128)(2,1)} %param.4) | copy-start | bytes 884740
  49.0 9.5 %collective-permute-start.4 = (bf16[2,6,6,512]{3,2,1,0:T(8,128)(2,1)S(1)}, bf16[2,6,6,512]{3,2,1,0:T(8,128)(2,1)S(1)}, u32[]{:S(2)}, u32[]{:S(2)}) collective-permute-start(bf16[2,6,6,512]{3,2,1,0:T(8,128)(2,1)S(1)} %copy.19), channel_id=1, source_target_pairs={{0,8},{8,16},{16,24},{24,32},{32,40},{40,48},{48,56},{56,64},{64,7... | collective-permute-start | bytes 221192 | tf_op jit(solution)/shard_map/ppermute | solution.py:18
  58.6 9.7 %collective-permute-start.5 = (bf16[2,3,24,512]{3,2,1,0:T(8,128)(2,1)S(1)}, bf16[2,3,24,512]{3,2,1,0:T(8,128)(2,1)S(1)}, u32[]{:S(2)}, u32[]{:S(2)}) collective-permute-start(bf16[2,3,24,512]{3,2,1,0:T(8,128)(2,1)S(1)} %fusion.14), channel_id=1, source_target_pairs={{0,1},{1,2},{2,3},{3,4},{4,5},{5,6},{6,7},{7,0},{8,9},{9,10},{10,1... | collective-permute-start | bytes 442376 | tf_op jit(solution)/shard_map/ppermute | solution.py:18
where the time goes:
time: 70.8 us; the launch traced here: 70.4 us
  starting transfers between devices  30.9 us (44%)
  waiting for transfers between devices  19.9 us (28%)
  local copies, waits for them, and re-layouts  9.97 us (14%)
  matrix products  6.99 us (10%)
  other arithmetic  2.32 us (3%)
    ppermute x6, starting transfers between devices, from_behind(): return lax.ppermute(value, axis, pairs)  30.9 us
    ppermute x6, waiting for transfers between devices, from_behind(): return lax.ppermute(value, axis, pairs)  19.9 us
    dot_general x1, matrix products, shards(): jnp.dot(attended.reshape(-1, width), w_out, preferred_element_type=jnp.fl...  2.08 us
    dot_general x1, matrix products, one_band(): jnp.einsum('whqk,wkhd->wqhd', weights, values, preferred_element_type=jnp...  2.03 us
    convert_element_type x1, local copies, waits for them, and re-layouts, one_band(): return result.astype(jnp.bfloat16).reshape(window_count, window_size, width)  1.99 us
    dot_general x1, matrix products, attend(): jnp.dot(normed.reshape(-1, width), w_qkv, preferred_element_type=jnp.floa...  1.54 us
  transfers between devices with their start and end apart: 6, of which 5 were waited for; matrix products, arithmetic and copies ran while one was open for 4% of the time, Pallas kernels for 0%

commit v1 on v0

v1 whole, which is shorter than its diff:
```python
import math

import jax
import jax.numpy as jnp
from jax import lax
from jax.experimental import pallas as pl
from jax.experimental.pallas import tpu as pltpu
from jax.sharding import PartitionSpec as P

HEADS = 16
WIN_H = 6
WIN_W = 12
SHIFT_H = 3
SHIFT_W = 6
LEVELS = 2
TILE = 8
MESH = pl.DeviceIdType.MESH
F32 = jnp.float32
BF16 = jnp.bfloat16

EAST, EAST_N, EAST_S = 0, 1, 2
WEST, WEST_N, WEST_S = 3, 4, 5
NORTH, SOUTH = 6, 7
WAYS = ((1, 0), (1, -1), (1, 1), (-1, 0), (-1, -1), (-1, 1), (0, -1), (0, 1))
EASTWARD = (EAST, EAST_N, EAST_S)
WESTWARD = (WEST, WEST_N, WEST_S)


def layer_norm(values):
    center = values - jnp.mean(values, axis=-1, keepdims=True)
    spread = jnp.mean(center * center, axis=-1, keepdims=True)
    return (center * lax.rsqrt(spread + 1e-05)).astype(BF16)


def attend(queries, key_vecs, values, bias):
    query_count, width = queries.shape
    key_count = key_vecs.shape[0]
    head_depth = width // HEADS
    scale = math.log2(math.e) / math.sqrt(head_depth)
    per_group = 128 // head_depth
    lane = lax.broadcasted_iota(jnp.int32, (1, 128), 1) // head_depth
    only = [(lane == head).astype(F32).astype(BF16) for head in range(per_group)]
    ones = jnp.ones((key_count, 128), BF16)
    sums, totals = [], []
    for group in range(width // 128):
        part = slice(group * 128, (group + 1) * 128)
        spread = jnp.concatenate([queries[:, part] * mask for mask in only], axis=0)
        scores = lax.dot_general(
            spread, key_vecs[:, part], (((1,), (1,)), ((), ())), preferred_element_type=F32
        )
        scores = scores.reshape(per_group, query_count, key_count)
        weights = jnp.exp2(scores * scale + bias[None]).astype(BF16)
        result = jnp.dot(
            weights.reshape(per_group * query_count, key_count),
            jnp.concatenate([values[:, part], ones], axis=1),
            preferred_element_type=F32,
        ).reshape(per_group, query_count, 256)
        chosen = result[per_group - 1]
        lanes = lax.broadcasted_iota(jnp.int32, (query_count, 256), 1) % 128 // head_depth
        for head in range(per_group - 1):
            chosen = jnp.where(lanes == head, result[head], chosen)
        sums.append(chosen[:, :128])
        totals.append(chosen[:, 128:])
    return jnp.concatenate(sums, axis=1), jnp.concatenate(totals, axis=1)


def bias_of(query_code, key_code):
    return jnp.where(query_code == key_code, F32(-8.0), F32(-1e30))


def row_code(ids, shape, dim, cols):
    col = lax.broadcasted_iota(jnp.int32, shape, dim) % cols
    code = jnp.broadcast_to(ids[0], shape)
    for block in range(1, 4):
        code = jnp.where(col >= block * SHIFT_W, ids[block] + 4 * ((block + 1) // 2), code)
    return code


def kernel(
    n_lon, n_lat,
    x_hbm, ids_hbm, w_qkv_hbm, w_out_hbm,
    out_ref,
    x, w_qkv, w_out, ids, north, south, east, west, halo_ids, queries, sums, totals,
    load_sem, send_sem, recv_sem, ready,
):
    lon, lat = lax.axis_index("lon"), lax.axis_index("lat")
    first, last, before = lon == 0, lon == n_lon - 1, lon == n_lon - 2
    has_north, has_south = lat > 0, lat < n_lat - 1
    more_north, more_south = jnp.where(has_north, 1, 0), jnp.where(has_south, 1, 0)
    three = 1 + more_north + more_south
    width = x.shape[-1]
    half_tokens = LEVELS * SHIFT_H * 3 * TILE

    def device(way):
        dlon, dlat = WAYS[way]
        return {"lon": lax.rem(lon + dlon + n_lon, n_lon), "lat": lax.rem(lat + dlat + n_lat, n_lat)}

    def exists(way):
        dlat = WAYS[way][1]
        return has_north if dlat < 0 else has_south if dlat > 0 else None

    def comes(way):
        dlat = WAYS[way][1]
        return has_south if dlat < 0 else has_north if dlat > 0 else None

    def when(condition, do):
        def run():
            do()

        if condition is None:
            run()
        else:
            pl.when(condition)(run)

    def signal_all(semaphore, ways):
        for way in ways:
            when(
                exists(way),
                lambda way=way: pl.semaphore_signal(
                    semaphore, inc=1, device_id=device(way), device_id_type=MESH
                ),
            )

    def rows_sent(way):
        return {0: pl.ds(0, 6), -1: pl.ds(0, 3), 1: pl.ds(3, 3)}[WAYS[way][1]]

    def copies(way):
        dlon, dlat = WAYS[way]
        rows = rows_sent(way)
        lands = {0: pl.ds(3, 6), -1: pl.ds(9, 3), 1: pl.ds(0, 3)}[dlat]
        if dlon == 0:
            pair = (x_hbm.at[:, rows], (south if dlat < 0 else north))
        elif dlon > 0:
            pair = (x_hbm.at[:, rows, 2], west.at[:, lands])
        else:
            pair = (x_hbm.at[:, rows, 0], east.at[:, lands])
        pairs = (pair, (ids_hbm, halo_ids.at[way]))
        return [
            pltpu.make_async_remote_copy(
                src_ref=source,
                dst_ref=target,
                send_sem=send_sem.at[way, part],
                recv_sem=recv_sem.at[way, part],
                device_id=device(way),
                device_id_type=MESH,
            )
            for part, (source, target) in enumerate(pairs)
        ]

    def send(ways):
        for way in ways:
            when(exists(way), lambda way=way: [copy.start() for copy in copies(way)])

    def wait_recv(ways):
        for way in ways:
            when(comes(way), lambda way=way: [copy.wait_recv() for copy in copies(way)])

    def wait_send(ways):
        for way in ways:
            when(exists(way), lambda way=way: [copy.wait_send() for copy in copies(way)])

    barrier = pltpu.get_barrier_semaphore()
    ready_east, ready_west, ready_south = ready.at[0], ready.at[1], ready.at[2]
    inner = jnp.logical_not(jnp.logical_or(first, last))
    to_east = jnp.logical_or(before, last)
    pl.when(jnp.logical_not(to_east))(lambda: signal_all(barrier, EASTWARD))
    pl.when(jnp.logical_not(inner))(lambda: signal_all(barrier, WESTWARD))
    pl.when(jnp.logical_not(last))(lambda: signal_all(barrier, (SOUTH,)))

    loads = [
        pltpu.make_async_copy(source, target, load_sem.at[index])
        for index, (source, target) in enumerate(
            ((x_hbm, x), (ids_hbm, ids), (w_qkv_hbm, w_qkv), (w_out_hbm, w_out))
        )
    ]
    for load in loads:
        load.start()

    greeted = (
        jnp.where(inner, three, 0)
        + jnp.where(to_east, three, 0)
        + jnp.where(jnp.logical_not(last), more_north, 0)
    )

    @pl.when(greeted > 0)
    def _():
        pl.semaphore_wait(barrier, greeted)

    @pl.when(to_east)
    def _():
        send((EAST_N, EAST_S, EAST))
        signal_all(ready_west, EASTWARD)

    @pl.when(inner)
    def _():
        signal_all(ready_east, WESTWARD)

    @pl.when(jnp.logical_not(last))
    def _():
        signal_all(ready_south, (NORTH,))

    @pl.when(inner)
    def _():
        send(WESTWARD)

    @pl.when(jnp.logical_not(last))
    def _():
        send((NORTH,))

    @pl.when(jnp.logical_not(has_north))
    def _():
        east[:, 0:3] = jnp.zeros((LEVELS, 3, TILE, width), BF16)
        west[:, 0:3] = jnp.zeros((LEVELS, 3, TILE, width), BF16)
        for way in (EAST_S, WEST_S):
            halo_ids[way] = jnp.zeros(halo_ids.shape[1:], jnp.int32)

    @pl.when(jnp.logical_not(has_south))
    def _():
        east[:, 9:12] = jnp.zeros((LEVELS, 3, TILE, width), BF16)
        west[:, 9:12] = jnp.zeros((LEVELS, 3, TILE, width), BF16)
        for way in (EAST_N, WEST_N):
            halo_ids[way] = jnp.zeros(halo_ids.shape[1:], jnp.int32)

    def class_of(ref, row, block):
        return ref[row, 0:1, block * SHIFT_W : block * SHIFT_W + 1]

    def classes(ref, row):
        return [class_of(ref, row, block) for block in range(4)]

    def query_code(half):
        return row_code(classes(ids, 3 * half), (half_tokens, 1), 0, 24)

    def halo_projection(source):
        normed = layer_norm(source.astype(F32).reshape(-1, width))
        both = jnp.dot(normed, w_qkv[:, width:], preferred_element_type=F32).astype(BF16)
        return both[:, :width], both[:, width:]

    for load in loads[:3]:
        load.wait()
    block = (LEVELS, 3, 3, TILE, width)
    for half in range(2):
        rows = slice(3 * half, 3 * half + 3)
        normed = layer_norm(x[:, rows].astype(F32).reshape(half_tokens, width))
        projected = jnp.dot(normed, w_qkv[...], preferred_element_type=F32)
        queries[:, rows] = projected[:, :width].reshape(block)
        projected = projected.astype(BF16)
        key_code = row_code(classes(ids, 3 * half), (1, half_tokens), 1, 24)
        some, total = attend(
            projected[:, :width],
            projected[:, width : 2 * width],
            projected[:, 2 * width :],
            bias_of(query_code(half), key_code),
        )
        sums[:, rows] = some.reshape(block)
        totals[:, rows] = total.reshape(block)

    @pl.when(jnp.logical_not(to_east))
    def _():
        pl.semaphore_wait(ready_east, three)
        send(EASTWARD)

    @pl.when(jnp.logical_and(jnp.logical_not(last), has_south))
    def _():
        pl.semaphore_wait(ready_south, 1)
        send((SOUTH,))

    @pl.when(last)
    def _():
        pl.semaphore_wait(ready_west, three)
        send((NORTH, SOUTH) + WESTWARD)

    def row_halo(half, source, way):
        rows = slice(3 * half, 3 * half + 3)
        key_vecs, values = halo_projection(source[...])
        key_code = row_code(classes(halo_ids.at[way], 3 - 3 * half), (1, half_tokens), 1, 24)
        some, total = attend(
            queries[:, rows].reshape(half_tokens, width).astype(BF16),
            key_vecs,
            values,
            bias_of(query_code(half), key_code),
        )
        sums[:, rows] += some.reshape(block)
        totals[:, rows] += total.reshape(block)

    @pl.when(has_north)
    def _():
        wait_recv((SOUTH,))
        row_halo(0, north, SOUTH)

    @pl.when(has_south)
    def _():
        wait_recv((NORTH,))
        row_halo(1, south, NORTH)

    def side_halo(tile, source, ways, query_block, key_block, query_cols, key_cols):
        straight, from_south, from_north = ways
        key_vecs, values = halo_projection(source[...])
        token = lax.broadcasted_iota(jnp.int32, (LEVELS * 6 * TILE, 1), 0)
        col, row = token % TILE, token // TILE % 6
        mine = jnp.where(
            row >= 3, class_of(ids, 3, query_block) + 4, class_of(ids, 0, query_block)
        )
        mine = jnp.where((col >= query_cols[0]) & (col < query_cols[1]), mine, -2)
        token = lax.broadcasted_iota(jnp.int32, (1, LEVELS * 12 * TILE), 1)
        col, row = token % TILE, token // TILE % 12
        theirs = jnp.where(
            row >= 9,
            class_of(halo_ids.at[from_south], 0, key_block) + 4,
            jnp.where(
                row >= 6,
                class_of(halo_ids.at[straight], 3, key_block) + 4,
                jnp.where(
                    row >= 3,
                    class_of(halo_ids.at[straight], 0, key_block),
                    class_of(halo_ids.at[from_north], 3, key_block),
                ),
            ),
        )
        seen = (col >= key_cols[0]) & (col < key_cols[1])
        seen = seen & ((row >= 3 * (1 - more_north)) & (row < 9 + 3 * more_south))
        theirs = jnp.where(seen, theirs, -1)
        some, total = attend(
            queries[:, :, tile].reshape(-1, width).astype(BF16), key_vecs, values, bias_of(mine, theirs)
        )
        side = (LEVELS, 6, TILE, width)
        return sums[:, :, tile] + some.reshape(side), totals[:, :, tile] + total.reshape(side)

    def finish(patches, some, total):
        attended = (some / total).astype(BF16).reshape(-1, width)
        output = jnp.dot(attended, w_out[...], preferred_element_type=F32)
        return (patches.astype(F32) + output.reshape(patches.shape)).astype(BF16)

    wait_recv(WESTWARD)
    some, total = side_halo(2, east, WESTWARD, 3, 0, (2, 8), (0, 6))
    loads[3].wait()
    out_ref[:, :, 2] = finish(x[:, :, 2], some, total)
    out_ref[:, :, 1] = finish(x[:, :, 1], sums[:, :, 1], totals[:, :, 1])

    @pl.when(first)
    def _():
        pl.semaphore_wait(ready_west, three)
        send(WESTWARD)

    wait_recv(EASTWARD)
    some, total = side_halo(0, west, EASTWARD, 0, 3, (0, 6), (2, 8))
    out_ref[:, :, 0] = finish(x[:, :, 0], some, total)

    wait_send(range(len(WAYS)))


def shards(n_lon, n_lat, patches, regions, w_qkv, w_out):
    levels, row_count, col_count, width = patches.shape
    tiles = (levels, row_count, col_count // TILE, TILE, width)
    half = (levels, SHIFT_H, col_count // TILE, TILE, width)
    side = (levels, row_count + 2 * SHIFT_H, TILE, width)
    id_shape = (row_count, levels, col_count)
    hbm = pl.BlockSpec(memory_space=pltpu.HBM)
    updated = pl.pallas_call(
        lambda *refs: kernel(n_lon, n_lat, *refs),
        out_shape=jax.ShapeDtypeStruct(tiles, BF16),
        in_specs=[hbm] * 4,
        out_specs=pl.BlockSpec(memory_space=pltpu.VMEM),
        scratch_shapes=[
            pltpu.VMEM(tiles, BF16),
            pltpu.VMEM(w_qkv.shape, BF16),
            pltpu.VMEM(w_out.shape, BF16),
            pltpu.VMEM(id_shape, jnp.int32),
            pltpu.VMEM(half, BF16),
            pltpu.VMEM(half, BF16),
            pltpu.VMEM(side, BF16),
            pltpu.VMEM(side, BF16),
            pltpu.VMEM((len(WAYS),) + id_shape, jnp.int32),
            pltpu.VMEM(tiles, F32),
            pltpu.VMEM(tiles, F32),
            pltpu.VMEM(tiles, F32),
            pltpu.SemaphoreType.DMA((4,)),
            pltpu.SemaphoreType.DMA((len(WAYS), 2)),
            pltpu.SemaphoreType.DMA((len(WAYS), 2)),
            pltpu.SemaphoreType.REGULAR((3,)),
        ],
        compiler_params=pltpu.CompilerParams(
            collective_id=0, has_side_effects=True, vmem_limit_bytes=60 * 2**20
        ),
    )(patches.reshape(tiles), regions.transpose(1, 0, 2), w_qkv, w_out)
    return updated.reshape(patches.shape)


def solution(mesh):
    n_lon, n_lat = mesh.shape["lon"], mesh.shape["lat"]
    return jax.shard_map(
        lambda *arrays: shards(n_lon, n_lat, *arrays),
        mesh=mesh,
        in_specs=(P(None, "lat", "lon", None), P(None, "lat", "lon"), P(), P()),
        out_specs=P(None, "lat", "lon", None),
        check_vma=False,
    )
```

time: 70.8 us -> 26 us (0.37)
  the two profiles are of different devices: /device:TPU:2 before, /device:TPU:483 now
where the time goes in v1:
time: 26 us; the launch traced here: 25.9 us
  Pallas kernels  24.2 us (93%)
  local copies, waits for them, and re-layouts  1.69 us (6%)
    pallas_call x1, Pallas kernels, shards(): pl.pallas_call(lambda *refs: kernel(n_lon, n_lat, *refs), out_shape=jax.S...  24.2 us
    unnamed x1, local copies, waits for them, and re-layouts  1.69 us

profile of v1, /device:TPU:483, one launch (start us, length us, event | category | flops | bytes accessed | tf_op | source)
XLA Modules:
  0.0 25.9 jit_solution(14384452497144997423)
XLA Ops:
  0.0 24.2 %shard_map.46 = bf16[2,6,3,8,512]{4,3,2,1,0:T(8,128)(2,1)} custom-call(bf16[2,6,3,8,512]{4,3,2,1,0:T(8,128)(2,1)} %bitcast.4, s32[6,2,24]{2,1,0:T(2,128)} %bitcast.5, bf16[512,1536]{1,0:T(8,128)(2,1)} %refs_2_.1, bf16[512,512]{1,0:T(8,128)(2,1)} %refs_3_.1), custom_call_target="tpu_custom_call" | custom-call | tf_op jit(solution)/shard_map/pallas_call | solution.py:358
  24.2 1.7 %copy.6 = bf16[2,6,24,512]{3,2,1,0:T(8,128)(2,1)} copy(bf16[2,6,24,512]{3,2,1,0:T(8,128)(2,1)} %bitcast.3) | data formatting | bytes 589824

commit v2 on v1

--- a/solution.py
+++ b/solution.py
@@ -80,19 +80,33 @@
     n_lon, n_lat,
     x_hbm, ids_hbm, w_qkv_hbm, w_out_hbm,
     out_ref,
-    x, w_qkv, w_out, ids, north, south, east, west, halo_ids, queries, sums, totals,
+    x, w_qkv, w_out, ids, beside, east, west, halo_ids, queries, sums, totals,
     load_sem, send_sem, recv_sem, ready,
 ):
     lon, lat = lax.axis_index("lon"), lax.axis_index("lat")
     first, last, before = lon == 0, lon == n_lon - 1, lon == n_lon - 2
+    even = lax.rem(lon, 2) == 0
+    odd = jnp.logical_not(even)
+    crossed_west = jnp.logical_and(even, jnp.logical_not(first))
+    crossed_east = jnp.logical_and(odd, jnp.logical_not(last))
+    north, south = beside.at[0], beside.at[1]
+
+    def east_first(lon):
+        late_corner = jnp.logical_and(lon == 1, lat == 0)
+        falling = jnp.logical_and(lax.rem(lon, 4) == 3, lon >= n_lon // 2)
+        return (lon >= n_lon - 2) | (lon < 0) | late_corner | falling
+
+    def south_first(lat):
+        late_corner = jnp.logical_and(lat == 0, lon < 2)
+        return jnp.logical_or(lax.rem(lat, n_lat // 2) == n_lat // 2 - 1, late_corner)
+
     has_north, has_south = lat > 0, lat < n_lat - 1
     more_north, more_south = jnp.where(has_north, 1, 0), jnp.where(has_south, 1, 0)
     three = 1 + more_north + more_south
     width = x.shape[-1]
     half_tokens = LEVELS * SHIFT_H * 3 * TILE
 
-    def device(way):
-        dlon, dlat = WAYS[way]
+    def device(dlon, dlat):
         return {"lon": lax.rem(lon + dlon + n_lon, n_lon), "lat": lax.rem(lat + dlat + n_lat, n_lat)}
 
     def exists(way):
@@ -117,55 +131,100 @@
             when(
                 exists(way),
                 lambda way=way: pl.semaphore_signal(
-                    semaphore, inc=1, device_id=device(way), device_id_type=MESH
+                    semaphore, inc=1, device_id=device(*WAYS[way]), device_id_type=MESH
                 ),
             )
 
-    def rows_sent(way):
-        return {0: pl.ds(0, 6), -1: pl.ds(0, 3), 1: pl.ds(3, 3)}[WAYS[way][1]]
-
-    def copies(way):
+    def message(way, sources, send_index, target):
         dlon, dlat = WAYS[way]
-        rows = rows_sent(way)
         lands = {0: pl.ds(3, 6), -1: pl.ds(9, 3), 1: pl.ds(0, 3)}[dlat]
         if dlon == 0:
-            pair = (x_hbm.at[:, rows], (south if dlat < 0 else north))
-        elif dlon > 0:
-            pair = (x_hbm.at[:, rows, 2], west.at[:, lands])
+            landing = south if dlat < 0 else north
         else:
-            pair = (x_hbm.at[:, rows, 0], east.at[:, lands])
-        pairs = (pair, (ids_hbm, halo_ids.at[way]))
+            landing = (west if dlon > 0 else east).at[:, lands]
         return [
             pltpu.make_async_remote_copy(
                 src_ref=source,
-                dst_ref=target,
-                send_sem=send_sem.at[way, part],
+                dst_ref=place,
+                send_sem=send_sem.at[send_index, part],
                 recv_sem=recv_sem.at[way, part],
-                device_id=device(way),
+                device_id=device(*target),
                 device_id_type=MESH,
             )
-            for part, (source, target) in enumerate(pairs)
+            for part, (source, place) in enumerate(zip(sources, (landing, halo_ids.at[way])))
         ]
+
+    def direct(way):
+        dlon, dlat = WAYS[way]
+        rows = {0: pl.ds(0, 6), -1: pl.ds(0, 3), 1: pl.ds(3, 3)}[dlat]
+        source = x_hbm.at[:, rows] if dlon == 0 else x_hbm.at[:, rows, 2 if dlon > 0 else 0]
+        return message(way, (source, ids_hbm), way, WAYS[way])
 
     def send(ways):
         for way in ways:
-            when(exists(way), lambda way=way: [copy.start() for copy in copies(way)])
+            when(exists(way), lambda way=way: [copy.start() for copy in direct(way)])
 
     def wait_recv(ways):
         for way in ways:
-            when(comes(way), lambda way=way: [copy.wait_recv() for copy in copies(way)])
+            when(comes(way), lambda way=way: [copy.wait_recv() for copy in direct(way)])
 
     def wait_send(ways):
         for way in ways:
-            when(exists(way), lambda way=way: [copy.wait_send() for copy in copies(way)])
+            when(exists(way), lambda way=way: [copy.wait_send() for copy in direct(way)])
+
+    def chip_relays(way):
+        source, edge = (north, has_north) if way == SOUTH else (south, has_south)
+        to_east, to_west = (EAST_S, WEST_S) if way == SOUTH else (EAST_N, WEST_N)
+        return [
+            (
+                jnp.logical_and(edge, even if dlon > 0 else odd),
+                message(to, (source.at[:, :, 2 if dlon > 0 else 0], halo_ids.at[way]), to, (dlon, 0)),
+            )
+            for to, dlon in ((to_east, 1), (to_west, -1))
+        ]
+
+    def lat_relays(way):
+        source = west if way == EAST else east
+        parts = (
+            (EAST_N if way == EAST else WEST_N, has_north, pl.ds(3, 3), -1),
+            (EAST_S if way == EAST else WEST_S, has_south, pl.ds(6, 3), 1),
+        )
+        crossed = crossed_west if way == EAST else crossed_east
+        return [
+            (
+                jnp.logical_and(edge, crossed),
+                message(to, (source.at[:, rows], halo_ids.at[way]), len(WAYS) + to, (0, dlat)),
+            )
+            for to, edge, rows, dlat in parts
+        ]
+
+    def start(relays):
+        for condition, copies in relays:
+            when(condition, lambda copies=copies: [copy.start() for copy in copies])
+
+    def finish_relays(relays):
+        for condition, copies in relays:
+            when(condition, lambda copies=copies: [copy.wait_send() for copy in copies])
 
     barrier = pltpu.get_barrier_semaphore()
-    ready_east, ready_west, ready_south = ready.at[0], ready.at[1], ready.at[2]
-    inner = jnp.logical_not(jnp.logical_or(first, last))
+    ready_east, ready_west, ready_north, ready_south = [ready.at[index] for index in range(4)]
     to_east = jnp.logical_or(before, last)
-    pl.when(jnp.logical_not(to_east))(lambda: signal_all(barrier, EASTWARD))
-    pl.when(jnp.logical_not(inner))(lambda: signal_all(barrier, WESTWARD))
-    pl.when(jnp.logical_not(last))(lambda: signal_all(barrier, (SOUTH,)))
+    not_last = jnp.logical_not(last)
+    early_east, early_west = east_first(lon), jnp.logical_not(east_first(lon - 1))
+    late_east, late_west = jnp.logical_not(early_east), jnp.logical_not(early_west)
+    inner_south = jnp.logical_and(has_south, not_last)
+    inner_north = jnp.logical_and(has_north, not_last)
+    early_south = jnp.logical_and(inner_south, south_first(lat))
+    late_south = jnp.logical_and(inner_south, jnp.logical_not(south_first(lat)))
+    early_north = jnp.logical_and(inner_north, jnp.logical_not(south_first(lat - 1)))
+    late_north = jnp.logical_and(inner_north, south_first(lat - 1))
+    seam = jnp.logical_or(first, last)
+
+    pl.when(late_east)(lambda: signal_all(barrier, (EAST,)))
+    pl.when(jnp.logical_and(late_west, jnp.logical_not(seam)))(lambda: signal_all(barrier, (WEST,)))
+    pl.when(seam)(lambda: signal_all(barrier, WESTWARD))
+    pl.when(late_south)(lambda: signal_all(barrier, (SOUTH,)))
+    pl.when(late_north)(lambda: signal_all(barrier, (NORTH,)))
 
     loads = [
         pltpu.make_async_copy(source, target, load_sem.at[index])
@@ -173,39 +232,50 @@
             ((x_hbm, x), (ids_hbm, ids), (w_qkv_hbm, w_qkv), (w_out_hbm, w_out))
         )
     ]
-    for load in loads:
-        load.start()
-
+
+    def start_loads():
+        for load in loads:
+            load.start()
+
+    pl.when(not_last)(start_loads)
     greeted = (
-        jnp.where(inner, three, 0)
-        + jnp.where(to_east, three, 0)
-        + jnp.where(jnp.logical_not(last), more_north, 0)
+        jnp.where(early_west, 1, 0)
+        + jnp.where(early_east, jnp.where(to_east, three, 1), 0)
+        + jnp.where(jnp.logical_or(early_north, early_south), 1, 0)
+        + jnp.where(jnp.logical_and(early_north, early_south), 1, 0)
     )
 
     @pl.when(greeted > 0)
     def _():
         pl.semaphore_wait(barrier, greeted)
 
-    @pl.when(to_east)
-    def _():
-        send((EAST_N, EAST_S, EAST))
-        signal_all(ready_west, EASTWARD)
-
-    @pl.when(inner)
-    def _():
-        signal_all(ready_east, WESTWARD)
-
-    @pl.when(jnp.logical_not(last))
+    @pl.when(last)
+    def _():
+        send((EAST_N, EAST_S))
+
+    @pl.when(early_east)
+    def _():
+        send((EAST,))
+
+    pl.when(last)(lambda: signal_all(ready_west, EASTWARD))
+    pl.when(jnp.logical_and(early_east, not_last))(lambda: signal_all(ready_west, (EAST,)))
+
+    pl.when(last)(start_loads)
+
+    @pl.when(early_west)
+    def _():
+        signal_all(ready_east, (WEST,))
+        send((WEST,))
+
+    @pl.when(early_north)
     def _():
         signal_all(ready_south, (NORTH,))
-
-    @pl.when(inner)
-    def _():
-        send(WESTWARD)
-
-    @pl.when(jnp.logical_not(last))
-    def _():
         send((NORTH,))
+
+    @pl.when(early_south)
+    def _():
+        signal_all(ready_north, (SOUTH,))
+        send((SOUTH,))
 
     @pl.when(jnp.logical_not(has_north))
     def _():
@@ -253,26 +323,48 @@
         )
         sums[:, rows] = some.reshape(block)
         totals[:, rows] = total.reshape(block)
-
-    @pl.when(jnp.logical_not(to_east))
-    def _():
-        pl.semaphore_wait(ready_east, three)
-        send(EASTWARD)
-
-    @pl.when(jnp.logical_and(jnp.logical_not(last), has_south))
-    def _():
-        pl.semaphore_wait(ready_south, 1)
-        send((SOUTH,))
-
-    @pl.when(last)
-    def _():
-        pl.semaphore_wait(ready_west, three)
-        send((NORTH, SOUTH) + WESTWARD)
-
-    def row_halo(half, source, way):
-        rows = slice(3 * half, 3 * half + 3)
-        key_vecs, values = halo_projection(source[...])
-        key_code = row_code(classes(halo_ids.at[way], 3 - 3 * half), (1, half_tokens), 1, 24)
+        if half == 0:
+
+            @pl.when(late_south)
+            def _():
+                pl.semaphore_wait(ready_south, 1)
+                send((SOUTH,))
+
+            @pl.when(late_north)
+            def _():
+                pl.semaphore_wait(ready_north, 1)
+                send((NORTH,))
+
+            @pl.when(last)
+            def _():
+                pl.semaphore_wait(ready_west, 1)
+                send((NORTH, SOUTH, WEST))
+
+    @pl.when(late_east)
+    def _():
+        pl.semaphore_wait(ready_east, 1)
+        send((EAST,))
+
+    @pl.when(jnp.logical_and(late_west, jnp.logical_not(seam)))
+    def _():
+        pl.semaphore_wait(ready_west, 1)
+        send((WEST,))
+
+    @pl.when(crossed_west)
+    def _():
+        wait_recv((EAST,))
+
+    @pl.when(crossed_east)
+    def _():
+        wait_recv((WEST,))
+
+    start(lat_relays(EAST) + lat_relays(WEST))
+
+    def row_halo(half):
+        rows = pl.ds(3 * half, 3)
+        key_vecs, values = halo_projection(beside[half])
+        their_ids = halo_ids.at[jnp.where(half == 0, SOUTH, NORTH)]
+        key_code = row_code(classes(their_ids, 3 - 3 * half), (1, half_tokens), 1, 24)
         some, total = attend(
             queries[:, rows].reshape(half_tokens, width).astype(BF16),
             key_vecs,
@@ -282,15 +374,23 @@
         sums[:, rows] += some.reshape(block)
         totals[:, rows] += total.reshape(block)
 
-    @pl.when(has_north)
-    def _():
-        wait_recv((SOUTH,))
-        row_halo(0, north, SOUTH)
-
-    @pl.when(has_south)
-    def _():
-        wait_recv((NORTH,))
-        row_halo(1, south, NORTH)
+    north_first = jnp.where(early_south, 1, 0)
+    for step in range(2):
+        half = 1 - north_first if step == 0 else north_first
+
+        @pl.when(half == 0)
+        def _():
+            wait_recv((SOUTH,))
+            start(chip_relays(SOUTH))
+
+        @pl.when(half == 1)
+        def _():
+            wait_recv((NORTH,))
+            start(chip_relays(NORTH))
+
+        @pl.when(jnp.where(half == 0, more_north, more_south) == 1)
+        def _():
+            row_halo(half)
 
     def side_halo(tile, source, ways, query_block, key_block, query_cols, key_cols):
         straight, from_south, from_north = ways
@@ -330,7 +430,11 @@
         output = jnp.dot(attended, w_out[...], preferred_element_type=F32)
         return (patches.astype(F32) + output.reshape(patches.shape)).astype(BF16)
 
-    wait_recv(WESTWARD)
+    @pl.when(jnp.logical_not(crossed_east))
+    def _():
+        wait_recv((WEST,))
+
+    wait_recv((WEST_N, WEST_S))
     some, total = side_halo(2, east, WESTWARD, 3, 0, (2, 8), (0, 6))
     loads[3].wait()
     out_ref[:, :, 2] = finish(x[:, :, 2], some, total)
@@ -341,11 +445,28 @@
         pl.semaphore_wait(ready_west, three)
         send(WESTWARD)
 
-    wait_recv(EASTWARD)
+    @pl.when(jnp.logical_not(crossed_west))
+    def _():
+        wait_recv((EAST,))
+
+    wait_recv((EAST_N, EAST_S))
     some, total = side_halo(0, west, EASTWARD, 0, 3, (0, 6), (2, 8))
     out_ref[:, :, 0] = finish(x[:, :, 0], some, total)
 
-    wait_send(range(len(WAYS)))
+    wait_send((EAST, WEST, NORTH, SOUTH))
+
+    @pl.when(last)
+    def _():
+        wait_send((EAST_N, EAST_S))
+
+    @pl.when(first)
+    def _():
+        wait_send((WEST_N, WEST_S))
+
+    for way in (NORTH, SOUTH):
+        finish_relays(chip_relays(way))
+    for way in (EAST, WEST):
+        finish_relays(lat_relays(way))
 
 
 def shards(n_lon, n_lat, patches, regions, w_qkv, w_out):
@@ -357,7 +478,7 @@
     hbm = pl.BlockSpec(memory_space=pltpu.HBM)
     updated = pl.pallas_call(
         lambda *refs: kernel(n_lon, n_lat, *refs),
-        out_shape=jax.ShapeDtypeStruct(tiles, BF16),
+        out_shape=pltpu.VMEM(tiles, BF16),
         in_specs=[hbm] * 4,
         out_specs=pl.BlockSpec(memory_space=pltpu.VMEM),
         scratch_shapes=[
@@ -365,8 +486,7 @@
             pltpu.VMEM(w_qkv.shape, BF16),
             pltpu.VMEM(w_out.shape, BF16),
             pltpu.VMEM(id_shape, jnp.int32),
-            pltpu.VMEM(half, BF16),
-            pltpu.VMEM(half, BF16),
+            pltpu.VMEM((2,) + half, BF16),
             pltpu.VMEM(side, BF16),
             pltpu.VMEM(side, BF16),
             pltpu.VMEM((len(WAYS),) + id_shape, jnp.int32),
@@ -374,9 +494,9 @@
             pltpu.VMEM(tiles, F32),
             pltpu.VMEM(tiles, F32),
             pltpu.SemaphoreType.DMA((4,)),
+            pltpu.SemaphoreType.DMA((2 * len(WAYS), 2)),
             pltpu.SemaphoreType.DMA((len(WAYS), 2)),
-            pltpu.SemaphoreType.DMA((len(WAYS), 2)),
-            pltpu.SemaphoreType.REGULAR((3,)),
+            pltpu.SemaphoreType.REGULAR((4,)),
         ],
         compiler_params=pltpu.CompilerParams(
             collective_id=0, has_side_effects=True, vmem_limit_bytes=60 * 2**20

time: 26 us -> 19.2 us (0.74)
  the two profiles are of different devices: /device:TPU:483 before, /device:TPU:9 now
where the time goes in v2:
time: 19.2 us; the launch traced here: 19.1 us
  Pallas kernels  18.4 us (96%)
  local copies, waits for them, and re-layouts  0.72 us (4%)
    pallas_call x1, Pallas kernels, shards(): pl.pallas_call(lambda *refs: kernel(n_lon, n_lat, *refs), out_shape=pltpu...  18.4 us
    unnamed x1, local copies, waits for them, and re-layouts  0.72 us

profile of v2, /device:TPU:9, one launch (start us, length us, event | category | flops | bytes accessed | tf_op | source)
XLA Modules:
  0.0 19.1 jit_solution(10135821664310366215)
XLA Ops:
  0.0 18.4 %shard_map.46 = bf16[2,6,3,8,512]{4,3,2,1,0:T(8,128)(2,1)S(1)} custom-call(bf16[2,6,3,8,512]{4,3,2,1,0:T(8,128)(2,1)} %bitcast.4, s32[6,2,24]{2,1,0:T(2,128)} %bitcast.5, bf16[512,1536]{1,0:T(8,128)(2,1)} %refs_2_.1, bf16[512,512]{1,0:T(8,128)(2,1)} %refs_3_.1), custom_call_target="tpu_custom_call" | custom-call | tf_op jit(solution)/shard_map/pallas_call | solution.py:479
  18.4 0.7 %copy.6 = bf16[2,6,24,512]{3,2,1,0:T(8,128)(2,1)} copy(bf16[2,6,24,512]{3,2,1,0:T(8,128)(2,1)S(1)} %bitcast.3) | data formatting | bytes 589824

commit v3 on v2

--- a/solution.py
+++ b/solution.py
@@ -14,6 +14,7 @@
 SHIFT_W = 6
 LEVELS = 2
 TILE = 8
+GROUP = 4
 MESH = pl.DeviceIdType.MESH
 F32 = jnp.float32
 BF16 = jnp.bfloat16
@@ -26,41 +27,30 @@
 WESTWARD = (WEST, WEST_N, WEST_S)
 
 
-def layer_norm(values):
-    center = values - jnp.mean(values, axis=-1, keepdims=True)
-    spread = jnp.mean(center * center, axis=-1, keepdims=True)
-    return (center * lax.rsqrt(spread + 1e-05)).astype(BF16)
-
-
 def attend(queries, key_vecs, values, bias):
-    query_count, width = queries.shape
+    width = queries.shape[1]
     key_count = key_vecs.shape[0]
     head_depth = width // HEADS
     scale = math.log2(math.e) / math.sqrt(head_depth)
-    per_group = 128 // head_depth
     lane = lax.broadcasted_iota(jnp.int32, (1, 128), 1) // head_depth
-    only = [(lane == head).astype(F32).astype(BF16) for head in range(per_group)]
-    ones = jnp.ones((key_count, 128), BF16)
+    only = [(lane == head).astype(F32).astype(BF16) for head in range(GROUP)]
+    ones = jnp.concatenate([jnp.broadcast_to(mask, (key_count, 128)) for mask in only], axis=0)
     sums, totals = [], []
     for group in range(width // 128):
         part = slice(group * 128, (group + 1) * 128)
-        spread = jnp.concatenate([queries[:, part] * mask for mask in only], axis=0)
         scores = lax.dot_general(
-            spread, key_vecs[:, part], (((1,), (1,)), ((), ())), preferred_element_type=F32
-        )
-        scores = scores.reshape(per_group, query_count, key_count)
-        weights = jnp.exp2(scores * scale + bias[None]).astype(BF16)
+            queries[:, part],
+            jnp.concatenate([key_vecs[:, part] * mask for mask in only], axis=0),
+            (((1,), (1,)), ((), ())),
+            preferred_element_type=F32,
+        )
+        weights = jnp.exp2(scores * scale + bias).astype(BF16)
+        spread = jnp.concatenate([values[:, part] * mask for mask in only], axis=0)
         result = jnp.dot(
-            weights.reshape(per_group * query_count, key_count),
-            jnp.concatenate([values[:, part], ones], axis=1),
-            preferred_element_type=F32,
-        ).reshape(per_group, query_count, 256)
-        chosen = result[per_group - 1]
-        lanes = lax.broadcasted_iota(jnp.int32, (query_count, 256), 1) % 128 // head_depth
-        for head in range(per_group - 1):
-            chosen = jnp.where(lanes == head, result[head], chosen)
-        sums.append(chosen[:, :128])
-        totals.append(chosen[:, 128:])
+            weights, jnp.concatenate([spread, ones], axis=1), preferred_element_type=F32
+        )
+        sums.append(result[:, :128])
+        totals.append(result[:, 128:])
     return jnp.concatenate(sums, axis=1), jnp.concatenate(totals, axis=1)
 
 
@@ -80,7 +70,7 @@
     n_lon, n_lat,
     x_hbm, ids_hbm, w_qkv_hbm, w_out_hbm,
     out_ref,
-    x, w_qkv, w_out, ids, beside, east, west, halo_ids, queries, sums, totals,
+    x, w_qkv, w_out, ids, beside, east, west, halo_ids, w_sums, queries, sums, totals,
     load_sem, send_sem, recv_sem, ready,
 ):
     lon, lat = lax.axis_index("lon"), lax.axis_index("lat")
@@ -88,16 +78,15 @@
     even = lax.rem(lon, 2) == 0
     odd = jnp.logical_not(even)
     crossed_west = jnp.logical_and(even, jnp.logical_not(first))
-    crossed_east = jnp.logical_and(odd, jnp.logical_not(last))
     north, south = beside.at[0], beside.at[1]
 
     def east_first(lon):
-        late_corner = jnp.logical_and(lon == 1, lat == 0)
+        late_corner = jnp.logical_and(lon == 0, lat == 0)
         falling = jnp.logical_and(lax.rem(lon, 4) == 3, lon >= n_lon // 2)
         return (lon >= n_lon - 2) | (lon < 0) | late_corner | falling
 
     def south_first(lat):
-        late_corner = jnp.logical_and(lat == 0, lon < 2)
+        late_corner = jnp.logical_and(lat == 0, lon == 0)
         return jnp.logical_or(lax.rem(lat, n_lat // 2) == n_lat // 2 - 1, late_corner)
 
     has_north, has_south = lat > 0, lat < n_lat - 1
@@ -137,11 +126,11 @@
 
     def message(way, sources, send_index, target):
         dlon, dlat = WAYS[way]
-        lands = {0: pl.ds(3, 6), -1: pl.ds(9, 3), 1: pl.ds(0, 3)}[dlat]
+        side = west if dlon > 0 else east
         if dlon == 0:
             landing = south if dlat < 0 else north
         else:
-            landing = (west if dlon > 0 else east).at[:, lands]
+            landing = side.at[0] if dlat == 0 else side.at[1, :, pl.ds(3 if dlat < 0 else 0, 3)]
         return [
             pltpu.make_async_remote_copy(
                 src_ref=source,
@@ -186,14 +175,14 @@
     def lat_relays(way):
         source = west if way == EAST else east
         parts = (
-            (EAST_N if way == EAST else WEST_N, has_north, pl.ds(3, 3), -1),
-            (EAST_S if way == EAST else WEST_S, has_south, pl.ds(6, 3), 1),
-        )
-        crossed = crossed_west if way == EAST else crossed_east
+            (EAST_N if way == EAST else WEST_N, has_north, pl.ds(0, 3), -1),
+            (EAST_S if way == EAST else WEST_S, has_south, pl.ds(3, 3), 1),
+        )
+        crossed = crossed_west if way == EAST else odd
         return [
             (
                 jnp.logical_and(edge, crossed),
-                message(to, (source.at[:, rows], halo_ids.at[way]), len(WAYS) + to, (0, dlat)),
+                message(to, (source.at[0, :, rows], halo_ids.at[way]), len(WAYS) + to, (0, dlat)),
             )
             for to, edge, rows, dlat in parts
         ]
@@ -251,43 +240,31 @@
 
     @pl.when(last)
     def _():
-        send((EAST_N, EAST_S))
-
-    @pl.when(early_east)
-    def _():
-        send((EAST,))
-
-    pl.when(last)(lambda: signal_all(ready_west, EASTWARD))
-    pl.when(jnp.logical_and(early_east, not_last))(lambda: signal_all(ready_west, (EAST,)))
-
-    pl.when(last)(start_loads)
-
-    @pl.when(early_west)
-    def _():
-        signal_all(ready_east, (WEST,))
-        send((WEST,))
-
-    @pl.when(early_north)
-    def _():
-        signal_all(ready_south, (NORTH,))
-        send((NORTH,))
-
-    @pl.when(early_south)
-    def _():
-        signal_all(ready_north, (SOUTH,))
-        send((SOUTH,))
+        signal_all(ready_west, (EAST,))
+        send((EAST_N, EAST_S, EAST))
+        start_loads()
+
+    inner_east = jnp.logical_and(early_east, not_last)
+    pl.when(early_north)(lambda: signal_all(ready_south, (NORTH,)))
+    pl.when(early_south)(lambda: signal_all(ready_north, (SOUTH,)))
+    pl.when(early_west)(lambda: signal_all(ready_east, (WEST,)))
+    pl.when(inner_east)(lambda: signal_all(ready_west, (EAST,)))
+    pl.when(early_west)(lambda: send((WEST,)))
+    pl.when(early_south)(lambda: send((SOUTH,)))
+    pl.when(early_north)(lambda: send((NORTH,)))
+    pl.when(inner_east)(lambda: send((EAST,)))
 
     @pl.when(jnp.logical_not(has_north))
     def _():
-        east[:, 0:3] = jnp.zeros((LEVELS, 3, TILE, width), BF16)
-        west[:, 0:3] = jnp.zeros((LEVELS, 3, TILE, width), BF16)
+        east[1, :, 0:3] = jnp.zeros((LEVELS, 3, TILE, width), BF16)
+        west[1, :, 0:3] = jnp.zeros((LEVELS, 3, TILE, width), BF16)
         for way in (EAST_S, WEST_S):
             halo_ids[way] = jnp.zeros(halo_ids.shape[1:], jnp.int32)
 
     @pl.when(jnp.logical_not(has_south))
     def _():
-        east[:, 9:12] = jnp.zeros((LEVELS, 3, TILE, width), BF16)
-        west[:, 9:12] = jnp.zeros((LEVELS, 3, TILE, width), BF16)
+        east[1, :, 3:6] = jnp.zeros((LEVELS, 3, TILE, width), BF16)
+        west[1, :, 3:6] = jnp.zeros((LEVELS, 3, TILE, width), BF16)
         for way in (EAST_N, WEST_N):
             halo_ids[way] = jnp.zeros(halo_ids.shape[1:], jnp.int32)
 
@@ -300,21 +277,31 @@
     def query_code(half):
         return row_code(classes(ids, 3 * half), (half_tokens, 1), 0, 24)
 
-    def halo_projection(source):
-        normed = layer_norm(source.astype(F32).reshape(-1, width))
-        both = jnp.dot(normed, w_qkv[:, width:], preferred_element_type=F32).astype(BF16)
+    def project(source, first_feature):
+        values = source.astype(F32).reshape(-1, width)
+        center = jnp.mean(values, axis=-1, keepdims=True)
+        spread = jnp.mean(jnp.square(values - center), axis=-1, keepdims=True)
+        product = jnp.dot(
+            values.astype(BF16), w_qkv[:, first_feature:], preferred_element_type=F32
+        )
+        return (product - center * w_sums[0:1, first_feature:]) * lax.rsqrt(spread + 1e-05)
+
+    def project_halo(source):
+        both = project(source, width).astype(BF16)
         return both[:, :width], both[:, width:]
 
     for load in loads[:3]:
         load.wait()
     block = (LEVELS, 3, 3, TILE, width)
+    w_sums[...] = jnp.dot(
+        jnp.ones((TILE, width), BF16), w_qkv[...], preferred_element_type=F32
+    )
     for half in range(2):
         rows = slice(3 * half, 3 * half + 3)
-        normed = layer_norm(x[:, rows].astype(F32).reshape(half_tokens, width))
-        projected = jnp.dot(normed, w_qkv[...], preferred_element_type=F32)
+        projected = project(x[:, rows], 0)
         queries[:, rows] = projected[:, :width].reshape(block)
         projected = projected.astype(BF16)
-        key_code = row_code(classes(ids, 3 * half), (1, half_tokens), 1, 24)
+        key_code = row_code(classes(ids, 3 * half), (1, GROUP * half_tokens), 1, 24)
         some, total = attend(
             projected[:, :width],
             projected[:, width : 2 * width],
@@ -330,11 +317,6 @@
                 pl.semaphore_wait(ready_south, 1)
                 send((SOUTH,))
 
-            @pl.when(late_north)
-            def _():
-                pl.semaphore_wait(ready_north, 1)
-                send((NORTH,))
-
             @pl.when(last)
             def _():
                 pl.semaphore_wait(ready_west, 1)
@@ -345,26 +327,21 @@
         pl.semaphore_wait(ready_east, 1)
         send((EAST,))
 
+    @pl.when(late_north)
+    def _():
+        pl.semaphore_wait(ready_north, 1)
+        send((NORTH,))
+
     @pl.when(jnp.logical_and(late_west, jnp.logical_not(seam)))
     def _():
         pl.semaphore_wait(ready_west, 1)
         send((WEST,))
 
-    @pl.when(crossed_west)
-    def _():
-        wait_recv((EAST,))
-
-    @pl.when(crossed_east)
-    def _():
-        wait_recv((WEST,))
-
-    start(lat_relays(EAST) + lat_relays(WEST))
-
     def row_halo(half):
         rows = pl.ds(3 * half, 3)
-        key_vecs, values = halo_projection(beside[half])
+        key_vecs, values = project_halo(beside[half])
         their_ids = halo_ids.at[jnp.where(half == 0, SOUTH, NORTH)]
-        key_code = row_code(classes(their_ids, 3 - 3 * half), (1, half_tokens), 1, 24)
+        key_code = row_code(classes(their_ids, 3 - 3 * half), (1, GROUP * half_tokens), 1, 24)
         some, total = attend(
             queries[:, rows].reshape(half_tokens, width).astype(BF16),
             key_vecs,
@@ -374,9 +351,64 @@
         sums[:, rows] += some.reshape(block)
         totals[:, rows] += total.reshape(block)
 
-    north_first = jnp.where(early_south, 1, 0)
+    def side_halo(tile, source, part, ways, query_block, key_block, query_cols, key_cols):
+        straight, from_south, from_north = ways
+        key_vecs, values = project_halo(source[part])
+        shape = (LEVELS * 6 * TILE, 1)
+        token = lax.broadcasted_iota(jnp.int32, shape, 0)
+        col, row = token % TILE, token // TILE % 6
+        mine = jnp.where(
+            row >= 3, class_of(ids, 3, query_block) + 4, class_of(ids, 0, query_block)
+        )
+        mine = jnp.where((col >= query_cols[0]) & (col < query_cols[1]), mine, -2)
+        token = lax.broadcasted_iota(jnp.int32, (1, GROUP * shape[0]), 1)
+        col, row = token % TILE, token // TILE % 6
+        corner = part == 1
+        upper = halo_ids.at[jnp.where(corner, from_north, straight)]
+        lower = halo_ids.at[jnp.where(corner, from_south, straight)]
+        theirs = jnp.where(
+            row >= 3,
+            class_of(lower, jnp.where(corner, 0, 3), key_block) + 4,
+            class_of(upper, jnp.where(corner, 3, 0), key_block),
+        )
+        seen = (col >= key_cols[0]) & (col < key_cols[1])
+        seen = seen & (row >= jnp.where(corner, 3 * (1 - more_north), 0))
+        seen = seen & (row < jnp.where(corner, 3 + 3 * more_south, 6))
+        some, total = attend(
+            queries[:, :, tile].reshape(-1, width).astype(BF16),
+            key_vecs,
+            values,
+            bias_of(mine, jnp.where(seen, theirs, -1)),
+        )
+        side = (LEVELS, 6, TILE, width)
+        sums[:, :, tile] += some.reshape(side)
+        totals[:, :, tile] += total.reshape(side)
+
+    def east_halo(part):
+        side_halo(2, east, part, WESTWARD, 3, 0, (2, 8), (0, 6))
+
+    def west_halo(part):
+        side_halo(0, west, part, EASTWARD, 0, 3, (0, 6), (2, 8))
+
+    def finish(tiles):
+        attended = (sums[:, :, tiles] / totals[:, :, tiles]).astype(BF16).reshape(-1, width)
+        output = jnp.dot(attended, w_out[...], preferred_element_type=F32)
+        patches = x[:, :, tiles].astype(F32)
+        out_ref[:, :, tiles] = (patches + output.reshape(patches.shape)).astype(BF16)
+
+    def relay_east():
+        wait_recv((WEST,))
+        start(lat_relays(WEST))
+
+    def relay_west():
+        wait_recv((EAST,))
+        start(lat_relays(EAST))
+
+    north_first = jnp.where(early_south | (last & south_first(lat)), 1, 0)
     for step in range(2):
         half = 1 - north_first if step == 0 else north_first
+        if step == 0:
+            pl.when(jnp.logical_and(odd, not_last))(relay_east)
 
         @pl.when(half == 0)
         def _():
@@ -388,80 +420,66 @@
             wait_recv((NORTH,))
             start(chip_relays(NORTH))
 
+        if step == 0:
+            pl.when(crossed_west)(relay_west)
+
         @pl.when(jnp.where(half == 0, more_north, more_south) == 1)
         def _():
             row_halo(half)
 
-    def side_halo(tile, source, ways, query_block, key_block, query_cols, key_cols):
-        straight, from_south, from_north = ways
-        key_vecs, values = halo_projection(source[...])
-        token = lax.broadcasted_iota(jnp.int32, (LEVELS * 6 * TILE, 1), 0)
-        col, row = token % TILE, token // TILE % 6
-        mine = jnp.where(
-            row >= 3, class_of(ids, 3, query_block) + 4, class_of(ids, 0, query_block)
-        )
-        mine = jnp.where((col >= query_cols[0]) & (col < query_cols[1]), mine, -2)
-        token = lax.broadcasted_iota(jnp.int32, (1, LEVELS * 12 * TILE), 1)
-        col, row = token % TILE, token // TILE % 12
-        theirs = jnp.where(
-            row >= 9,
-            class_of(halo_ids.at[from_south], 0, key_block) + 4,
-            jnp.where(
-                row >= 6,
-                class_of(halo_ids.at[straight], 3, key_block) + 4,
-                jnp.where(
-                    row >= 3,
-                    class_of(halo_ids.at[straight], 0, key_block),
-                    class_of(halo_ids.at[from_north], 3, key_block),
-                ),
-            ),
-        )
-        seen = (col >= key_cols[0]) & (col < key_cols[1])
-        seen = seen & ((row >= 3 * (1 - more_north)) & (row < 9 + 3 * more_south))
-        theirs = jnp.where(seen, theirs, -1)
-        some, total = attend(
-            queries[:, :, tile].reshape(-1, width).astype(BF16), key_vecs, values, bias_of(mine, theirs)
-        )
-        side = (LEVELS, 6, TILE, width)
-        return sums[:, :, tile] + some.reshape(side), totals[:, :, tile] + total.reshape(side)
-
-    def finish(patches, some, total):
-        attended = (some / total).astype(BF16).reshape(-1, width)
-        output = jnp.dot(attended, w_out[...], preferred_element_type=F32)
-        return (patches.astype(F32) + output.reshape(patches.shape)).astype(BF16)
-
-    @pl.when(jnp.logical_not(crossed_east))
-    def _():
-        wait_recv((WEST,))
+        if step == 0:
+
+            @pl.when(odd)
+            def _():
+                wait_recv((EAST,))
+
+            pl.when(jnp.logical_not(first))(lambda: west_halo(0))
+
+            @pl.when(even)
+            def _():
+                wait_recv((WEST,))
+
+            pl.when(last)(relay_east)
+            east_halo(0)
+
+    @pl.when(first)
+    def _():
+        pl.semaphore_wait(ready_west, 1)
+        send((WEST,))
 
     wait_recv((WEST_N, WEST_S))
-    some, total = side_halo(2, east, WESTWARD, 3, 0, (2, 8), (0, 6))
+    east_halo(1)
     loads[3].wait()
-    out_ref[:, :, 2] = finish(x[:, :, 2], some, total)
-    out_ref[:, :, 1] = finish(x[:, :, 1], sums[:, :, 1], totals[:, :, 1])
-
-    @pl.when(first)
-    def _():
-        pl.semaphore_wait(ready_west, three)
-        send(WESTWARD)
-
-    @pl.when(jnp.logical_not(crossed_west))
+    finish(slice(1, 3))
+    straight_first = first & has_north & (lax.rem(lat, n_lat // 2) == 0)
+    corners_first = jnp.logical_not(straight_first)
+
+    @pl.when(straight_first)
     def _():
         wait_recv((EAST,))
 
-    wait_recv((EAST_N, EAST_S))
-    some, total = side_halo(0, west, EASTWARD, 0, 3, (0, 6), (2, 8))
-    out_ref[:, :, 0] = finish(x[:, :, 0], some, total)
+    @pl.when(corners_first)
+    def _():
+        wait_recv((EAST_N, EAST_S))
+
+    pl.when(first)(lambda: west_halo(jnp.where(straight_first, 0, 1)))
+
+    @pl.when(straight_first)
+    def _():
+        wait_recv((EAST_N, EAST_S))
+
+    @pl.when(jnp.logical_and(first, corners_first))
+    def _():
+        wait_recv((EAST,))
+
+    west_halo(jnp.where(jnp.logical_and(first, corners_first), 0, 1))
+    finish(slice(0, 1))
 
     wait_send((EAST, WEST, NORTH, SOUTH))
 
     @pl.when(last)
     def _():
         wait_send((EAST_N, EAST_S))
-
-    @pl.when(first)
-    def _():
-        wait_send((WEST_N, WEST_S))
 
     for way in (NORTH, SOUTH):
         finish_relays(chip_relays(way))
@@ -473,7 +491,7 @@
     levels, row_count, col_count, width = patches.shape
     tiles = (levels, row_count, col_count // TILE, TILE, width)
     half = (levels, SHIFT_H, col_count // TILE, TILE, width)
-    side = (levels, row_count + 2 * SHIFT_H, TILE, width)
+    side = (2, levels, row_count, TILE, width)
     id_shape = (row_count, levels, col_count)
     hbm = pl.BlockSpec(memory_space=pltpu.HBM)
     updated = pl.pallas_call(
@@ -490,6 +508,7 @@
             pltpu.VMEM(side, BF16),
             pltpu.VMEM(side, BF16),
             pltpu.VMEM((len(WAYS),) + id_shape, jnp.int32),
+            pltpu.VMEM((TILE, w_qkv.shape[1]), F32),
             pltpu.VMEM(tiles, F32),
             pltpu.VMEM(tiles, F32),
             pltpu.VMEM(tiles, F32),

time: 19.2 us -> 18.8 us (0.979)
  the two profiles are of different devices: /device:TPU:9 before, /device:TPU:2 now
where the time goes in v3:
time: 18.8 us; the launch traced here: 18.6 us
  Pallas kernels  17.9 us (95%)
  local copies, waits for them, and re-layouts  0.72 us (4%)
    pallas_call x1, Pallas kernels, shards(): pl.pallas_call(lambda *refs: kernel(n_lon, n_lat, *refs), out_shape=pltpu...  17.9 us
    unnamed x1, local copies, waits for them, and re-layouts  0.72 us

profile of v3, /device:TPU:2, one launch (start us, length us, event | category | flops | bytes accessed | tf_op | source)
XLA Modules:
  0.0 18.6 jit_solution(8029108943863418133)
XLA Ops:
  0.0 17.9 %shard_map.46 = bf16[2,6,3,8,512]{4,3,2,1,0:T(8,128)(2,1)S(1)} custom-call(bf16[2,6,3,8,512]{4,3,2,1,0:T(8,128)(2,1)} %bitcast.4, s32[6,2,24]{2,1,0:T(2,128)} %bitcast.5, bf16[512,1536]{1,0:T(8,128)(2,1)} %refs_2_.1, bf16[512,512]{1,0:T(8,128)(2,1)} %refs_3_.1), custom_call_target="tpu_custom_call" | custom-call | tf_op jit(solution)/shard_map/pallas_call | solution.py:497
  17.9 0.7 %copy.6 = bf16[2,6,24,512]{3,2,1,0:T(8,128)(2,1)} copy(bf16[2,6,24,512]{3,2,1,0:T(8,128)(2,1)S(1)} %bitcast.3) | data formatting | bytes 589824

commit v4 on v3

--- a/solution.py
+++ b/solution.py
@@ -27,31 +27,49 @@
 WESTWARD = (WEST, WEST_N, WEST_S)
 
 
-def attend(queries, key_vecs, values, bias):
-    width = queries.shape[1]
-    key_count = key_vecs.shape[0]
+def attend(sets):
+    width = sets[0][0].shape[1]
     head_depth = width // HEADS
     scale = math.log2(math.e) / math.sqrt(head_depth)
     lane = lax.broadcasted_iota(jnp.int32, (1, 128), 1) // head_depth
     only = [(lane == head).astype(F32).astype(BF16) for head in range(GROUP)]
-    ones = jnp.concatenate([jnp.broadcast_to(mask, (key_count, 128)) for mask in only], axis=0)
-    sums, totals = [], []
-    for group in range(width // 128):
-        part = slice(group * 128, (group + 1) * 128)
-        scores = lax.dot_general(
+    parts = [slice(group * 128, (group + 1) * 128) for group in range(width // 128)]
+
+    def repeated(vectors):
+        return jnp.concatenate([vectors * mask for mask in only], axis=0)
+
+    scores = [
+        lax.dot_general(
             queries[:, part],
-            jnp.concatenate([key_vecs[:, part] * mask for mask in only], axis=0),
+            repeated(key_vecs[:, part]),
             (((1,), (1,)), ((), ())),
             preferred_element_type=F32,
         )
-        weights = jnp.exp2(scores * scale + bias).astype(BF16)
-        spread = jnp.concatenate([values[:, part] * mask for mask in only], axis=0)
-        result = jnp.dot(
-            weights, jnp.concatenate([spread, ones], axis=1), preferred_element_type=F32
-        )
-        sums.append(result[:, :128])
-        totals.append(result[:, 128:])
-    return jnp.concatenate(sums, axis=1), jnp.concatenate(totals, axis=1)
+        for queries, key_vecs, _, _ in sets
+        for part in parts
+    ]
+    weights = [
+        jnp.exp2(score * scale + sets[index // len(parts)][3]).astype(BF16)
+        for index, score in enumerate(scores)
+    ]
+    found = []
+    for index, (_, key_vecs, values, _) in enumerate(sets):
+        ones = repeated(jnp.ones((key_vecs.shape[0], 128), BF16))
+        results = [
+            jnp.dot(
+                weights[index * len(parts) + group],
+                jnp.concatenate([repeated(values[:, part]), ones], axis=1),
+                preferred_element_type=F32,
+            )
+            for group, part in enumerate(parts)
+        ]
+        found.append(
+            (
+                jnp.concatenate([result[:, :128] for result in results], axis=1),
+                jnp.concatenate([result[:, 128:] for result in results], axis=1),
+            )
+        )
+    return found
 
 
 def bias_of(query_code, key_code):
@@ -286,10 +304,6 @@
         )
         return (product - center * w_sums[0:1, first_feature:]) * lax.rsqrt(spread + 1e-05)
 
-    def project_halo(source):
-        both = project(source, width).astype(BF16)
-        return both[:, :width], both[:, width:]
-
     for load in loads[:3]:
         load.wait()
     block = (LEVELS, 3, 3, TILE, width)
@@ -302,11 +316,15 @@
         queries[:, rows] = projected[:, :width].reshape(block)
         projected = projected.astype(BF16)
         key_code = row_code(classes(ids, 3 * half), (1, GROUP * half_tokens), 1, 24)
-        some, total = attend(
-            projected[:, :width],
-            projected[:, width : 2 * width],
-            projected[:, 2 * width :],
-            bias_of(query_code(half), key_code),
+        ((some, total),) = attend(
+            [
+                (
+                    projected[:, :width],
+                    projected[:, width : 2 * width],
+                    projected[:, 2 * width :],
+                    bias_of(query_code(half), key_code),
+                )
+            ]
         )
         sums[:, rows] = some.reshape(block)
         totals[:, rows] = total.reshape(block)
@@ -339,50 +357,53 @@
 
     def row_halo(half):
         rows = pl.ds(3 * half, 3)
-        key_vecs, values = project_halo(beside[half])
+        both = project(beside[half], width).astype(BF16)
+        key_vecs, values = both[:, :width], both[:, width:]
         their_ids = halo_ids.at[jnp.where(half == 0, SOUTH, NORTH)]
         key_code = row_code(classes(their_ids, 3 - 3 * half), (1, GROUP * half_tokens), 1, 24)
-        some, total = attend(
-            queries[:, rows].reshape(half_tokens, width).astype(BF16),
-            key_vecs,
-            values,
-            bias_of(query_code(half), key_code),
+        ((some, total),) = attend(
+            [
+                (
+                    queries[:, rows].reshape(half_tokens, width).astype(BF16),
+                    key_vecs,
+                    values,
+                    bias_of(query_code(half), key_code),
+                )
+            ]
         )
         sums[:, rows] += some.reshape(block)
         totals[:, rows] += total.reshape(block)
 
     def side_halo(tile, source, part, ways, query_block, key_block, query_cols, key_cols):
         straight, from_south, from_north = ways
-        key_vecs, values = project_halo(source[part])
-        shape = (LEVELS * 6 * TILE, 1)
-        token = lax.broadcasted_iota(jnp.int32, shape, 0)
-        col, row = token % TILE, token // TILE % 6
-        mine = jnp.where(
-            row >= 3, class_of(ids, 3, query_block) + 4, class_of(ids, 0, query_block)
-        )
-        mine = jnp.where((col >= query_cols[0]) & (col < query_cols[1]), mine, -2)
-        token = lax.broadcasted_iota(jnp.int32, (1, GROUP * shape[0]), 1)
-        col, row = token % TILE, token // TILE % 6
         corner = part == 1
-        upper = halo_ids.at[jnp.where(corner, from_north, straight)]
-        lower = halo_ids.at[jnp.where(corner, from_south, straight)]
-        theirs = jnp.where(
-            row >= 3,
-            class_of(lower, jnp.where(corner, 0, 3), key_block) + 4,
-            class_of(upper, jnp.where(corner, 3, 0), key_block),
-        )
-        seen = (col >= key_cols[0]) & (col < key_cols[1])
-        seen = seen & (row >= jnp.where(corner, 3 * (1 - more_north), 0))
-        seen = seen & (row < jnp.where(corner, 3 + 3 * more_south, 6))
-        some, total = attend(
-            queries[:, :, tile].reshape(-1, width).astype(BF16),
-            key_vecs,
-            values,
-            bias_of(mine, jnp.where(seen, theirs, -1)),
-        )
-        side = (LEVELS, 6, TILE, width)
-        sums[:, :, tile] += some.reshape(side)
-        totals[:, :, tile] += total.reshape(side)
+        tokens = LEVELS * 3 * TILE
+        side = (LEVELS, 3, TILE, width)
+        both = project(source[part], width).reshape(LEVELS, 6, TILE, 2 * width)
+        query_col = lax.broadcasted_iota(jnp.int32, (tokens, 1), 0) % TILE
+        key_col = lax.broadcasted_iota(jnp.int32, (1, GROUP * tokens), 1) % TILE
+        sets = []
+        for half, way, exists_there in ((0, from_north, more_north), (1, from_south, more_south)):
+            rows = slice(3 * half, 3 * half + 3)
+            there = halo_ids.at[jnp.where(corner, way, straight)]
+            theirs = class_of(there, jnp.where(corner, 3 - 3 * half, 3 * half), key_block)
+            theirs = jnp.where(jnp.logical_and(corner, exists_there == 0), -1, theirs)
+            key_code = jnp.where((key_col >= key_cols[0]) & (key_col < key_cols[1]), theirs, -1)
+            mine = class_of(ids, 3 * half, query_block)
+            in_window = (query_col >= query_cols[0]) & (query_col < query_cols[1])
+            vectors = both[:, rows].reshape(tokens, 2 * width).astype(BF16)
+            sets.append(
+                (
+                    queries[:, rows, tile].reshape(tokens, width).astype(BF16),
+                    vectors[:, :width],
+                    vectors[:, width:],
+                    bias_of(jnp.where(in_window, mine, -2), key_code),
+                )
+            )
+        for half, (some, total) in enumerate(attend(sets)):
+            rows = slice(3 * half, 3 * half + 3)
+            sums[:, rows, tile] += some.reshape(side)
+            totals[:, rows, tile] += total.reshape(side)
 
     def east_halo(part):
         side_halo(2, east, part, WESTWARD, 3, 0, (2, 8), (0, 6))
@@ -409,6 +430,7 @@
         half = 1 - north_first if step == 0 else north_first
         if step == 0:
             pl.when(jnp.logical_and(odd, not_last))(relay_east)
+            pl.when(jnp.logical_and(crossed_west, north_first == 1))(relay_west)
 
         @pl.when(half == 0)
         def _():
@@ -420,27 +442,29 @@
             wait_recv((NORTH,))
             start(chip_relays(NORTH))
 
-        if step == 0:
-            pl.when(crossed_west)(relay_west)
-
         @pl.when(jnp.where(half == 0, more_north, more_south) == 1)
         def _():
             row_halo(half)
 
         if step == 0:
 
+            @pl.when(even)
+            def _():
+                wait_recv((WEST,))
+
+            pl.when(not_last)(lambda: east_halo(0))
+            pl.when(jnp.logical_and(crossed_west, north_first == 0))(relay_west)
+
             @pl.when(odd)
             def _():
                 wait_recv((EAST,))
 
             pl.when(jnp.logical_not(first))(lambda: west_halo(0))
 
-            @pl.when(even)
+            @pl.when(last)
             def _():
-                wait_recv((WEST,))
-
-            pl.when(last)(relay_east)
-            east_halo(0)
+                relay_east()
+                east_halo(0)
 
     @pl.when(first)
     def _():
@@ -451,30 +475,6 @@
     east_halo(1)
     loads[3].wait()
     finish(slice(1, 3))
-    straight_first = first & has_north & (lax.rem(lat, n_lat // 2) == 0)
-    corners_first = jnp.logical_not(straight_first)
-
-    @pl.when(straight_first)
-    def _():
-        wait_recv((EAST,))
-
-    @pl.when(corners_first)
-    def _():
-        wait_recv((EAST_N, EAST_S))
-
-    pl.when(first)(lambda: west_halo(jnp.where(straight_first, 0, 1)))
-
-    @pl.when(straight_first)
-    def _():
-        wait_recv((EAST_N, EAST_S))
-
-    @pl.when(jnp.logical_and(first, corners_first))
-    def _():
-        wait_recv((EAST,))
-
-    west_halo(jnp.where(jnp.logical_and(first, corners_first), 0, 1))
-    finish(slice(0, 1))
-
     wait_send((EAST, WEST, NORTH, SOUTH))
 
     @pl.when(last)
@@ -485,6 +485,30 @@
         finish_relays(chip_relays(way))
     for way in (EAST, WEST):
         finish_relays(lat_relays(way))
+
+    straight_first = first & has_north & (lax.rem(lat, n_lat // 2) == 0)
+    corners_first = jnp.logical_not(straight_first)
+
+    @pl.when(straight_first)
+    def _():
+        wait_recv((EAST,))
+
+    @pl.when(corners_first)
+    def _():
+        wait_recv((EAST_N, EAST_S))
+
+    pl.when(first)(lambda: west_halo(jnp.where(straight_first, 0, 1)))
+
+    @pl.when(straight_first)
+    def _():
+        wait_recv((EAST_N, EAST_S))
+
+    @pl.when(jnp.logical_and(first, corners_first))
+    def _():
+        wait_recv((EAST,))
+
+    west_halo(jnp.where(jnp.logical_and(first, corners_first), 0, 1))
+    finish(slice(0, 1))
 
 
 def shards(n_lon, n_lat, patches, regions, w_qkv, w_out):

time: 18.8 us -> 18.6 us (0.989)
  Pallas kernels: 17.9 us -> 17.7 us
where the time goes in v4:
time: 18.6 us; the launch traced here: 18.5 us
  Pallas kernels  17.7 us (95%)
  local copies, waits for them, and re-layouts  0.72 us (4%)
    pallas_call x1, Pallas kernels, shards(): pl.pallas_call(lambda *refs: kernel(n_lon, n_lat, *refs), out_shape=pltpu...  17.7 us
    unnamed x1, local copies, waits for them, and re-layouts  0.72 us

profile of v4, /device:TPU:2, one launch (start us, length us, event | category | flops | bytes accessed | tf_op | source)
XLA Modules:
  0.0 18.5 jit_solution(8613025991034431849)
XLA Ops:
  0.0 17.7 %shard_map.46 = bf16[2,6,3,8,512]{4,3,2,1,0:T(8,128)(2,1)S(1)} custom-call(bf16[2,6,3,8,512]{4,3,2,1,0:T(8,128)(2,1)} %bitcast.4, s32[6,2,24]{2,1,0:T(2,128)} %bitcast.5, bf16[512,1536]{1,0:T(8,128)(2,1)} %refs_2_.1, bf16[512,512]{1,0:T(8,128)(2,1)} %refs_3_.1), custom_call_target="tpu_custom_call" | custom-call | tf_op jit(solution)/shard_map/pallas_call | solution.py:521
  17.7 0.7 %copy.6 = bf16[2,6,24,512]{3,2,1,0:T(8,128)(2,1)} copy(bf16[2,6,24,512]{3,2,1,0:T(8,128)(2,1)S(1)} %bitcast.3) | data formatting | bytes 589824

commit v5 on v4

--- a/solution.py
+++ b/solution.py
@@ -229,7 +229,7 @@
 
     pl.when(late_east)(lambda: signal_all(barrier, (EAST,)))
     pl.when(jnp.logical_and(late_west, jnp.logical_not(seam)))(lambda: signal_all(barrier, (WEST,)))
-    pl.when(seam)(lambda: signal_all(barrier, WESTWARD))
+    pl.when(first)(lambda: signal_all(barrier, WESTWARD))
     pl.when(late_south)(lambda: signal_all(barrier, (SOUTH,)))
     pl.when(late_north)(lambda: signal_all(barrier, (NORTH,)))
 
@@ -260,6 +260,7 @@
     def _():
         signal_all(ready_west, (EAST,))
         send((EAST_N, EAST_S, EAST))
+        signal_all(barrier, WESTWARD)
         start_loads()
 
     inner_east = jnp.logical_and(early_east, not_last)
@@ -374,7 +375,9 @@
         sums[:, rows] += some.reshape(block)
         totals[:, rows] += total.reshape(block)
 
-    def side_halo(tile, source, part, ways, query_block, key_block, query_cols, key_cols):
+    def side_halo(
+        tile, source, part, ways, query_block, key_block, query_cols, key_cols, store=True
+    ):
         straight, from_south, from_north = ways
         corner = part == 1
         tokens = LEVELS * 3 * TILE
@@ -400,16 +403,23 @@
                     bias_of(jnp.where(in_window, mine, -2), key_code),
                 )
             )
+        found = []
         for half, (some, total) in enumerate(attend(sets)):
             rows = slice(3 * half, 3 * half + 3)
-            sums[:, rows, tile] += some.reshape(side)
-            totals[:, rows, tile] += total.reshape(side)
+            some = sums[:, rows, tile] + some.reshape(side)
+            total = totals[:, rows, tile] + total.reshape(side)
+            if not store:
+                found.append((some / total).astype(BF16).reshape(tokens, width))
+                continue
+            sums[:, rows, tile] = some
+            totals[:, rows, tile] = total
+        return found
 
     def east_halo(part):
         side_halo(2, east, part, WESTWARD, 3, 0, (2, 8), (0, 6))
 
-    def west_halo(part):
-        side_halo(0, west, part, EASTWARD, 0, 3, (0, 6), (2, 8))
+    def west_halo(part, store=True):
+        return side_halo(0, west, part, EASTWARD, 0, 3, (0, 6), (2, 8), store)
 
     def finish(tiles):
         attended = (sums[:, :, tiles] / totals[:, :, tiles]).astype(BF16).reshape(-1, width)
@@ -459,7 +469,10 @@
             def _():
                 wait_recv((EAST,))
 
-            pl.when(jnp.logical_not(first))(lambda: west_halo(0))
+            @pl.when(jnp.logical_not(first))
+            def _():
+                west_halo(0)
+
 
             @pl.when(last)
             def _():
@@ -497,7 +510,10 @@
     def _():
         wait_recv((EAST_N, EAST_S))
 
-    pl.when(first)(lambda: west_halo(jnp.where(straight_first, 0, 1)))
+    @pl.when(first)
+    def _():
+        west_halo(jnp.where(straight_first, 0, 1))
+
 
     @pl.when(straight_first)
     def _():
@@ -507,8 +523,14 @@
     def _():
         wait_recv((EAST,))
 
-    west_halo(jnp.where(jnp.logical_and(first, corners_first), 0, 1))
-    finish(slice(0, 1))
+    attended = west_halo(jnp.where(jnp.logical_and(first, corners_first), 0, 1), store=False)
+    output = jnp.dot(jnp.concatenate(attended, axis=0), w_out[...], preferred_element_type=F32)
+    tokens = output.shape[0] // 2
+    for half in range(2):
+        rows = slice(3 * half, 3 * half + 3)
+        patches = x[:, rows, 0].astype(F32)
+        new = output[half * tokens : (half + 1) * tokens].reshape(patches.shape)
+        out_ref[:, rows, 0] = (patches + new).astype(BF16)
 
 
 def shards(n_lon, n_lat, patches, regions, w_qkv, w_out):

time: 18.6 us -> 18.6 us (level)
  no operation moved by 1% of the time
where the time goes in v5:
time: 18.6 us; the launch traced here: 18.4 us
  Pallas kernels  17.7 us (95%)
  local copies, waits for them, and re-layouts  0.72 us (4%)
    pallas_call x1, Pallas kernels, shards(): pl.pallas_call(lambda *refs: kernel(n_lon, n_lat, *refs), out_shape=pltpu...  17.7 us
    unnamed x1, local copies, waits for them, and re-layouts  0.72 us

profile of v5, /device:TPU:2, one launch (start us, length us, event | category | flops | bytes accessed | tf_op | source)
XLA Modules:
  0.0 18.4 jit_solution(9676223226179854981)
XLA Ops:
  0.0 17.7 %shard_map.46 = bf16[2,6,3,8,512]{4,3,2,1,0:T(8,128)(2,1)S(1)} custom-call(bf16[2,6,3,8,512]{4,3,2,1,0:T(8,128)(2,1)} %bitcast.4, s32[6,2,24]{2,1,0:T(2,128)} %bitcast.5, bf16[512,1536]{1,0:T(8,128)(2,1)} %refs_2_.1, bf16[512,512]{1,0:T(8,128)(2,1)} %refs_3_.1), custom_call_target="tpu_custom_call" | custom-call | tf_op jit(solution)/shard_map/pallas_call | solution.py:543
  17.7 0.7 %copy.6 = bf16[2,6,24,512]{3,2,1,0:T(8,128)(2,1)} copy(bf16[2,6,24,512]{3,2,1,0:T(8,128)(2,1)S(1)} %bitcast.3) | data formatting | bytes 589824
